TPU v7x, 256 devices: a whole 4x4x8 slice. The times are simulated.
256 devices in a mesh: region: 8 (over x, core), sector: 32 (over z, y).
Axes of the slice: x: 4, y: 4, z: 8, core: 2. Of those that a mesh axis runs over, the one named last changes fastest.
Arguments:
- start_state: bfloat16 [8, 128, 128, 4, 128], P('region', 'sector'), may hold values from -6 to 6
- left_env: bfloat16 [8, 128, 16, 128, 128], P('region', 'sector'), may hold values from -0.125 to 0.125
- right_env: bfloat16 [8, 128, 16, 128, 128], P('region', 'sector'), may hold values from -0.5 to 0.5
- mpo_tensor: bfloat16 [16, 4, 4, 16], replicated, may hold values from -0.75 to 0.75
- decay: float32 [8, 128, 128], P('region', 'sector'), may hold values from 0.15 to 1
- energy_terms: float32 [8, 128, 128], P('region', 'sector'), may hold values from -1.2 to 1.2
- live_count: int32 [8, 32], P('region', 'sector'), may hold values from 1 to 4, as said below
Outputs:
- state_out: bfloat16 [8, 128, 128, 4, 128], P('region', 'sector')
- density: float32 [8, 128, 128, 128], P('region', 'sector')
- energy: float32 [8], P('region')
Inputs may be any that keep to these rules, and one draw needn't show every extreme that they name: `live_count`: each device's live blocks fill its first slots; some device holds 4 live blocks.
All inputs are finite; a program needn't handle non-finite values.
Results may differ from a plain program's by a relative error of at most 0.0055.
The roundings to bfloat16 on the way count: a program that leaves them out, or rounds other values in their place, can miss the bound.
Values may be sent and summed in bfloat16 or wider, within the bound.
No kernel may reach another device: no remote copies, remote signals or barrier semaphores. Data moves between devices by JAX's collectives and lax.ppermute only.
A program may use at most 64 MiB of HBM per device.

v0:
```python
import math

import jax
import jax.numpy as jnp
import numpy as np
from jax import lax
from jax.experimental import pallas as pl
from jax.experimental.pallas import tpu as pltpu
from jax.sharding import PartitionSpec as P

DAV = 2
EPS = 1e-06
BLK = 128
PHYS = 4
CHAN = 16
ROWS = BLK * PHYS
GROUP = 4
STRIDE = 8

(NORM, SHIFT, RES, BACK, DIAG, DEEP, ON_F, ON_R, ON_D) = range(9)


def constants():
    lanes = np.zeros((4 * BLK, 4 * BLK), np.float32)
    for u in range(4):
        for a in range(BLK):
            lanes[u * BLK + a, (a // GROUP) * 16 + u * GROUP + a % GROUP] = 1.0
    rows = np.zeros((256, 64), np.float32)
    cols = np.zeros((64, 256), np.float32)
    same = np.zeros((256, 256), np.float32)
    for s in range(PHYS):
        for u in range(CHAN):
            for g in range(GROUP):
                rows[s * 64 + u * GROUP + g, u * PHYS + s] = 1.0
    for t in range(PHYS):
        for w in range(CHAN):
            for g in range(GROUP):
                cols[t * CHAN + w, w * 16 + g * PHYS + t] = 1.0
    index = np.arange(256)
    same[:, :] = (index[:, None] % GROUP) == ((index[None, :] // PHYS) % GROUP)
    return [jnp.asarray(m, jnp.bfloat16) for m in (lanes, rows, cols, same)]


def matmul(x, y):
    return jnp.dot(x, y, preferred_element_type=jnp.float32)


def total(x):
    return jnp.sum(jnp.sum(x, axis=0, keepdims=True), axis=1, keepdims=True)


def ratio(top, bottom):
    return jnp.where(bottom > 0.0, top / jnp.where(bottom > 0.0, bottom, 1.0), 0.0)


def krylov_kernel(
    live_ref, region_ref, start_ref, own_ref, left_ref, right_ref, mpo_ref, offset_ref,
    lanes_ref, rows_ref, cols_ref, same_ref,
    res_ref, deep_ref, sums_ref,
    operator, left_lanes, first_half, second_half, spread, shift, sums,
):
    slot = pl.program_id(0)

    @pl.when(slot == 0)
    def _():
        wide = matmul(rows_ref[...], mpo_ref[...]).astype(jnp.bfloat16)
        wide = matmul(wide, cols_ref[...]).astype(jnp.bfloat16)
        operator[...] = wide * same_ref[...]
        sums[...] = jnp.zeros_like(sums)

    def operate(vector):
        for pair in range(CHAN // 2):
            right = jnp.concatenate([right_ref[0, 2 * pair], right_ref[0, 2 * pair + 1]], axis=1)
            made = matmul(vector, right).astype(jnp.bfloat16)
            for j in range(2):
                w = 2 * pair + j
                for half in range(2):
                    part = made[half * 256:(half + 1) * 256, j * BLK:(j + 1) * BLK]
                    first_half[:, w * 16:(w + 1) * 16, half * BLK:(half + 1) * BLK] = part.reshape(16, 16, BLK)
        for g in range(16):
            made = matmul(operator[...], first_half[g]).astype(jnp.bfloat16)
            for half in range(2):
                for s in range(PHYS):
                    for ug in range(4):
                        at = ug * 512 + (half * 16 + g) * 16
                        second_half[at:at + 16, s * BLK:(s + 1) * BLK] = made[
                            s * 64 + ug * 16:s * 64 + ug * 16 + 16, half * BLK:(half + 1) * BLK]
        made = matmul(left_lanes[...], second_half[...])
        for s in range(PHYS):
            spread[pl.ds(s, BLK, stride=PHYS), :] = made[:, s * BLK:(s + 1) * BLK]
        return spread[...]

    def order_lanes(ref):
        for ug in range(4):
            four = jnp.concatenate([ref[0, 4 * ug + j] for j in range(4)], axis=1)
            left_lanes[:, ug * 512:(ug + 1) * 512] = matmul(four, lanes_ref[...]).astype(jnp.bfloat16)

    live = live_ref[0, 0]
    outer = region_ref[0] == 0

    @pl.when(jnp.logical_and(slot < live, outer))
    def _():
        order_lanes(own_ref)

    @pl.when(jnp.logical_and(slot < live, jnp.logical_not(outer)))
    def _():
        order_lanes(left_ref)

    @pl.when(slot < live)
    def _():
        column = jnp.broadcast_to(offset_ref[pl.ds(slot, 1), :], (BLK, BLK)).T
        for s in range(PHYS):
            shift[pl.ds(s, BLK, stride=PHYS), :] = column
        lane = lax.broadcasted_iota(jnp.int32, (1, BLK), 1)

        def note(quantity, value):
            sums[...] += jnp.where(lane == quantity * STRIDE + slot, value, 0.0)

        first = start_ref[0].astype(jnp.float32)
        image = operate(start_ref[0]) + shift[...] * first
        norm = total(first * first)
        quotient = ratio(total(first * image), norm)
        res = image - quotient * first
        res_ref[0] = res
        res_norm = total(res * res)
        note(NORM, norm)
        note(SHIFT, quotient)
        note(RES, res_norm)

        vector = res_ref[0].astype(jnp.bfloat16)
        image = operate(vector) + shift[...] * vector.astype(jnp.float32)
        first = start_ref[0].astype(jnp.float32)
        res = res_ref[0]
        back = ratio(total(first * image), norm)
        diag = ratio(total(res * image), res_norm)
        deep = image - back * first - diag * res
        deep_ref[0] = deep
        note(BACK, back)
        note(DIAG, diag)
        note(DEEP, total(deep * deep))

        vector = deep_ref[0].astype(jnp.bfloat16)
        image = operate(vector) + shift[...] * vector.astype(jnp.float32)
        note(ON_F, total(start_ref[0].astype(jnp.float32) * image))
        note(ON_R, total(res_ref[0] * image))
        note(ON_D, total(deep_ref[0] * image))

    sums_ref[...] = jnp.broadcast_to(sums[...], sums_ref.shape)


def rotate_kernel(
    scale, sectors, live_ref, all_ref, own_ref, start_ref, res_ref, deep_ref,
    state_ref, density_ref, energy_ref, spread,
):
    table = jnp.concatenate([all_ref[...], own_ref[...]], axis=0)
    shape = (sectors + own_ref.shape[0], BLK)
    row = lax.broadcasted_iota(jnp.int32, shape, 0)
    lane = lax.broadcasted_iota(jnp.int32, shape, 1)
    counted = jnp.logical_and(row < sectors, lane < STRIDE)

    def pick(quantity):
        return table if quantity == 0 else pltpu.roll(table, BLK - quantity * STRIDE, 1)

    def region_sum(x):
        return total(jnp.where(counted, x, 0.0))

    norm, shift, res_norm, back, diag, deep_norm, on_f, on_r, on_d = [pick(k) for k in range(9)]
    grams = (norm, res_norm, deep_norm)
    zero = jnp.zeros(shape, jnp.float32)

    def inner(x, y):
        made = x[0] * y[0] * grams[0]
        for k in (1, 2):
            made = made + x[k] * y[k] * grams[k]
        if len(y) > 3:
            made = made + y[3] * (x[0] * on_f + x[1] * on_r + x[2] * on_d)
        return region_sum(made)

    inverse = lax.rsqrt(region_sum(norm) + EPS)
    current = (zero + inverse, zero, zero)
    applied = (inverse * shift, zero + inverse, zero)
    for iteration in range(DAV):
        quotient = inner(current, applied)
        residual = tuple(x - quotient * y for x, y in zip(applied, current))
        resid_sq = inner(residual, residual)
        factor = lax.rsqrt(resid_sq + EPS)
        search = tuple(factor * x for x in residual)
        image = (search[0] * shift + search[1] * back, search[0] + search[1] * diag, search[1])
        if iteration == 1:
            image = image + (search[2],)
        curvature = inner(search, image)
        opposite = -2.0 * resid_sq * factor
        adjacent = curvature - quotient
        largest = jnp.maximum(jnp.abs(opposite), jnp.abs(adjacent))
        flat = largest == 0.0
        largest = jnp.where(flat, 1.0, largest)
        opposite = opposite / largest
        adjacent = jnp.where(flat, 1.0, adjacent / largest)
        length = jnp.sqrt(opposite * opposite + adjacent * adjacent)
        double_cos = jnp.abs(adjacent) / length
        double_sin = jnp.abs(opposite) / length
        large = jnp.sqrt(0.5 + 0.5 * double_cos)
        small = double_sin / (2.0 * large)
        ahead = adjacent >= 0.0
        cos_part = jnp.where(ahead, large, small)
        sin_part = -jnp.where(ahead, small, large)
        current = tuple(cos_part * x + sin_part * y for x, y in zip(current, search))
        turned = tuple(cos_part * x + sin_part * y for x, y in zip(applied, image))
        applied = turned + tuple(sin_part * y for y in image[3:])
    energy_ref[...] = jnp.broadcast_to(inner(current, applied), energy_ref.shape)
    mine = [scale * x[sectors:sectors + 1, :] for x in current]
    live = live_ref[0, 0]
    for slot in range(start_ref.shape[0]):

        @pl.when(slot < live)
        def _():
            on_first, on_res, on_deep = [x[:, slot:slot + 1] for x in mine]
            state = on_first * start_ref[slot].astype(jnp.float32)
            state = state + on_res * res_ref[slot] + on_deep * deep_ref[slot]
            state = state.astype(jnp.bfloat16)
            state_ref[slot] = state
            spread[...] = state.astype(jnp.float32)
            wide = jnp.concatenate(
                [spread[pl.ds(s, BLK, stride=PHYS), :] for s in range(PHYS)], axis=1
            ).astype(jnp.bfloat16)
            product = lax.dot_general(
                wide, wide, (((1,), (1,)), ((), ())), preferred_element_type=jnp.float32
            )
            density_ref[slot] = product * (1.0 / ROWS)

        @pl.when(slot >= live)
        def _():
            state_ref[slot] = jnp.zeros(state_ref.shape[1:], state_ref.dtype)
            density_ref[slot] = jnp.zeros(density_ref.shape[1:], density_ref.dtype)


def from_behind(shard, axis, by):
    length = lax.axis_size(axis)
    return lax.ppermute(shard, axis, [(i, i + by) for i in range(length - by)])


def entering(decay, terms, axis):
    pair = from_behind(jnp.stack([decay, terms]), axis, 1)
    by = 1
    while by < lax.axis_size(axis):
        earlier = from_behind(pair, axis, by)
        pair = jnp.stack([pair[0] * earlier[0], pair[0] * earlier[1] + pair[1]])
        by *= 2
    return pair[1]


def body(start_state, left_env, right_env, mpo_tensor, decay, energy_terms, live_count):
    slots = start_state.shape[1]
    sectors = lax.axis_size("sector")
    start = start_state.reshape(slots, ROWS, BLK)
    arrived = from_behind(left_env[0], "region", 1)
    offsets = entering(decay[0], energy_terms[0], "region")
    region = lax.axis_index("region").reshape(1).astype(jnp.int32)
    mpo = mpo_tensor.reshape(CHAN * PHYS, PHYS * CHAN)

    def block(*shape):
        return pl.BlockSpec((1,) + shape, lambda n: (n,) + (0,) * len(shape))

    def whole(*shape):
        return pl.BlockSpec(shape, lambda n: (0,) * len(shape))

    smem = pl.BlockSpec(memory_space=pltpu.SMEM)
    res, deep, sums = pl.pallas_call(
        krylov_kernel,
        grid=(slots,),
        in_specs=[
            smem, smem, block(ROWS, BLK), block(CHAN, BLK, BLK), block(CHAN, BLK, BLK),
            block(CHAN, BLK, BLK), whole(64, 64), whole(slots, BLK),
            whole(512, 512), whole(256, 64), whole(64, 256), whole(256, 256),
        ],
        out_specs=[block(ROWS, BLK), block(ROWS, BLK), whole(sectors, BLK)],
        out_shape=[
            jax.ShapeDtypeStruct((slots, ROWS, BLK), jnp.float32),
            jax.ShapeDtypeStruct((slots, ROWS, BLK), jnp.float32),
            jax.ShapeDtypeStruct((sectors, BLK), jnp.float32),
        ],
        scratch_shapes=[
            pltpu.VMEM((256, 256), jnp.bfloat16),
            pltpu.VMEM((BLK, CHAN * BLK), jnp.bfloat16),
            pltpu.VMEM((16, 256, 256), jnp.bfloat16),
            pltpu.VMEM((CHAN * BLK, ROWS), jnp.bfloat16),
            pltpu.VMEM((ROWS, BLK), jnp.float32),
            pltpu.VMEM((ROWS, BLK), jnp.float32),
            pltpu.VMEM((1, BLK), jnp.float32),
        ],
        compiler_params=pltpu.CompilerParams(vmem_limit_bytes=40 << 20),
        name="krylov",
    )(live_count, region, start, left_env[0], arrived, right_env[0], mpo, offsets, *constants())
    every = lax.all_to_all(sums.reshape(sectors, 1, BLK), "sector", 0, 0).reshape(sectors, BLK)
    vmem = pl.BlockSpec(memory_space=pltpu.VMEM)
    state, density, energy = pl.pallas_call(
        lambda *refs: rotate_kernel(math.sqrt(slots * sectors * ROWS * BLK), sectors, *refs),
        in_specs=[smem] + [vmem] * 5,
        out_specs=[vmem] * 3,
        out_shape=[
            jax.ShapeDtypeStruct((slots, ROWS, BLK), jnp.bfloat16),
            jax.ShapeDtypeStruct((slots, BLK, BLK), jnp.float32),
            jax.ShapeDtypeStruct((1, 1), jnp.float32),
        ],
        scratch_shapes=[pltpu.VMEM((ROWS, BLK), jnp.float32)],
        compiler_params=pltpu.CompilerParams(vmem_limit_bytes=24 << 20),
        name="rotate",
    )(live_count, every, sums[:8], start, res, deep)
    return (state.reshape(start_state.shape), density[None], energy.reshape(1))


def solution(mesh):
    in_specs = (
        P("region", "sector", None, None, None),
        P("region", "sector", None, None, None),
        P("region", "sector", None, None, None),
        P(),
        P("region", "sector", None),
        P("region", "sector", None),
        P("region", "sector"),
    )
    out_specs = (
        P("region", "sector", None, None, None),
        P("region", "sector", None, None),
        P("region"),
    )
    return jax.shard_map(body, mesh=mesh, in_specs=in_specs, out_specs=out_specs, check_vma=False)
```

profile of v0, /device:TPU:6, one launch (start us, length us, event | category | flops | bytes accessed | tf_op | source)
XLA Modules:
  0.0 106.1 jit_solution(11771393912061673958)
XLA Ops:
  0.6 1.9 %collective-permute-start = (bf16[4,16,128,128]{3,2,1,0:T(8,128)(2,1)}, bf16[4,16,128,128]{3,2,1,0:T(8,128)(2,1)S(1)}, u32[]{:S(2)}, u32[]{:S(2)}) collective-permute-start(bf16[4,16,128,128]{3,2,1,0:T(8,128)(2,1)} %bitcast.13), channel_id=1, source_target_pairs={{0,32},{32,64},{64,96},{96,128},{128,160},{160,192},{192,224},{1,3... | collective-permute-start | bytes 6291464 | tf_op jit(solution)/shard_map/ppermute | solution.py:239
  2.6 0.7 pad_maximum_fusion
  3.3 1.9 %collective-permute-start.1 = (f32[2,4,128]{2,1,0:T(4,128)S(1)}, f32[2,4,128]{2,1,0:T(4,128)S(1)}, u32[]{:S(2)}, u32[]{:S(2)}) collective-permute-start(f32[2,4,128]{2,1,0:T(4,128)S(1)} %pad_maximum_fusion), channel_id=1, source_target_pairs={{0,32},{32,64},{64,96},{96,128},{128,160},{160,192},{192,224},{1,3... | collective-permute-start | bytes 12296 | tf_op jit(solution)/shard_map/ppermute | solution.py:239
  5.2 23.1 %collective-permute-done.1 = f32[2,4,128]{2,1,0:T(4,128)S(1)} collective-permute-done((f32[2,4,128]{2,1,0:T(4,128)S(1)}, f32[2,4,128]{2,1,0:T(4,128)S(1)}, u32[]{:S(2)}, u32[]{:S(2)}) %collective-permute-start.1) | collective-permute-done | bytes 4128 | tf_op jit(solution)/shard_map/ppermute | solution.py:239
  28.2 1.9 %collective-permute-start.2 = (f32[2,4,128]{2,1,0:T(4,128)S(1)}, f32[2,4,128]{2,1,0:T(4,128)S(1)}, u32[]{:S(2)}, u32[]{:S(2)}) collective-permute-start(f32[2,4,128]{2,1,0:T(4,128)S(1)} %collective-permute-done.1), channel_id=1, source_target_pairs={{0,32},{32,64},{64,96},{96,128},{128,160},{160,192},{192,224},{1,3... | collective-permute-start | bytes 12296 | tf_op jit(solution)/shard_map/ppermute | solution.py:239
  30.2 3.0 %collective-permute-done.2 = f32[2,4,128]{2,1,0:T(4,128)S(1)} collective-permute-done((f32[2,4,128]{2,1,0:T(4,128)S(1)}, f32[2,4,128]{2,1,0:T(4,128)S(1)}, u32[]{:S(2)}, u32[]{:S(2)}) %collective-permute-start.2) | collective-permute-done | bytes 4128 | tf_op jit(solution)/shard_map/ppermute | solution.py:239
  33.2 1.3 %collective-permute-start.3 = (f32[2,4,128]{2,1,0:T(4,128)S(1)}, f32[2,4,128]{2,1,0:T(4,128)S(1)}, u32[]{:S(2)}, u32[]{:S(2)}) collective-permute-start(f32[2,4,128]{2,1,0:T(4,128)S(1)} %pad_maximum_fusion.1), channel_id=1, source_target_pairs={{0,64},{32,96},{64,128},{96,160},{128,192},{160,224},{1,65},{33,97... | collective-permute-start | bytes 12296 | tf_op jit(solution)/shard_map/ppermute | solution.py:239
  34.5 4.2 %collective-permute-done.3 = f32[2,4,128]{2,1,0:T(4,128)S(1)} collective-permute-done((f32[2,4,128]{2,1,0:T(4,128)S(1)}, f32[2,4,128]{2,1,0:T(4,128)S(1)}, u32[]{:S(2)}, u32[]{:S(2)}) %collective-permute-start.3) | collective-permute-done | bytes 4128 | tf_op jit(solution)/shard_map/ppermute | solution.py:239
  38.7 1.3 %collective-permute-start.4 = (f32[2,4,128]{2,1,0:T(4,128)S(1)}, f32[2,4,128]{2,1,0:T(4,128)S(1)}, u32[]{:S(2)}, u32[]{:S(2)}) collective-permute-start(f32[2,4,128]{2,1,0:T(4,128)S(1)} %pad_maximum_fusion.2), channel_id=1, source_target_pairs={{0,128},{32,160},{64,192},{96,224},{1,129},{33,161},{65,193},{97,2... | collective-permute-start | bytes 12296 | tf_op jit(solution)/shard_map/ppermute | solution.py:239
  40.6 0.9 reshape.37.mpo_ref
  41.6 4.1 %collective-permute-done.4 = f32[2,4,128]{2,1,0:T(4,128)S(1)} collective-permute-done((f32[2,4,128]{2,1,0:T(4,128)S(1)}, f32[2,4,128]{2,1,0:T(4,128)S(1)}, u32[]{:S(2)}, u32[]{:S(2)}) %collective-permute-start.4) | collective-permute-done | bytes 4128 | tf_op jit(solution)/shard_map/ppermute | solution.py:239
  45.7 0.0 collective-permute-done.left_ref
  45.7 0.0 copy-start
  45.7 1.6 %copy-done = bf16[1,4,16,128,128]{4,3,2,1,0:T(8,128)(2,1)S(1)} copy-done((bf16[1,4,16,128,128]{4,3,2,1,0:T(8,128)(2,1)S(1)}, bf16[1,4,16,128,128]{4,3,2,1,0:T(8,128)(2,1)}, u32[]{:S(2)}) %copy-start) | copy-done | bytes 2097176
  47.3 0.0 copy-start.1
  47.3 1.6 %copy-done.1 = bf16[1,4,16,128,128]{4,3,2,1,0:T(8,128)(2,1)S(1)} copy-done((bf16[1,4,16,128,128]{4,3,2,1,0:T(8,128)(2,1)S(1)}, bf16[1,4,16,128,128]{4,3,2,1,0:T(8,128)(2,1)}, u32[]{:S(2)}) %copy-start.1) | copy-done | bytes 2097176
  48.9 0.0 copy-start.2
  48.9 1.0 copy-done.2
  49.9 1.0 copy-done.8
  51.0 0.9 copy-done.9
  51.9 0.8 copy-done.10
  52.7 0.8 copy-done.11
  53.5 7.2 %krylov.1 = (f32[4,512,128]{2,1,0:T(8,128)S(1)}, f32[4,512,128]{2,1,0:T(8,128)S(1)}, f32[32,128]{1,0:T(8,128)}) custom-call(s32[1,1]{1,0:T(1,128)S(6)} %copy.15.live_ref.refs_0_, s32[1]{0:T(128)} %bitcast.region_ref, bf16[4,512,128]{2,1,0:T(8,128)(2,1)S(1)} %bitcast.16, bf16[4,16,128,128]{3,2,1,0:T(8,128)(2,1)S(1)} %bitcast.14, ...), custom_call_target="tpu_custom_call" | custom-call | tf_op jit(solution)/shard_map/krylov/pallas_call | solution.py:268
  60.6 1.0 copy-done.4
  61.6 1.0 copy-done.6
  62.6 29.3 %all-to-all-start = ((f32[32,1,128]{2,1,0:T(1,128)}), f32[32,1,128]{2,1,0:T(1,128)S(1)}, u32[]{:S(2)}, u32[]{:S(2)}) async-start(f32[32,1,128]{2,1,0:T(1,128)} %bitcast.6), calls=%async_computation | async-start | bytes 32768 | tf_op jit(solution)/shard_map/all_to_all | solution.py:294
  91.8 0.7 slice.32.refs_2_
  92.6 9.0 %all-to-all-done = f32[32,1,128]{2,1,0:T(1,128)S(1)} async-done(((f32[32,1,128]{2,1,0:T(1,128)}), f32[32,1,128]{2,1,0:T(1,128)S(1)}, u32[]{:S(2)}, u32[]{:S(2)}) %all-to-all-start) | async-done | bytes 16416 | tf_op jit(solution)/shard_map/all_to_all | solution.py:294
  101.5 0.0 copy-done.3
  101.5 1.2 %copy-done.5 = f32[4,512,128]{2,1,0:T(8,128)S(1)} copy-done((f32[4,512,128]{2,1,0:T(8,128)S(1)}, f32[4,512,128]{2,1,0:T(8,128)}, u32[]{:S(2)}) %copy-start.5) | copy-done | bytes 1048600
  102.7 1.2 %copy-done.7 = f32[4,512,128]{2,1,0:T(8,128)S(1)} copy-done((f32[4,512,128]{2,1,0:T(8,128)S(1)}, f32[4,512,128]{2,1,0:T(8,128)}, u32[]{:S(2)}) %copy-start.7) | copy-done | bytes 1048600
  104.0 2.1 %rotate.1 = (bf16[4,512,128]{2,1,0:T(8,128)(2,1)}, f32[4,128,128]{2,1,0:T(8,128)}, f32[1,1]{1,0:T(1,128)}) custom-call(s32[1,1]{1,0:T(1,128)S(6)} %copy.15.live_ref.refs_0_, f32[32,128]{1,0:T(8,128)S(1)} %bitcast.18, f32[8,128]{1,0:T(8,128)S(1)} %slice.32.refs_2_, bf16[4,512,128]{2,1,0:T(8,128)(2,1)S(1)} %bitcast.17, f32[4,512,128]{2,1,0:T(8,128)S(1)} %copy-done.5, ...), custom_call_target="tpu_custom_call" | custom-call | tf_op jit(solution)/shard_map/rotate/pallas_call | solution.py:296
  (14 shorter events, 0.0 us)
Async XLA Ops:
  0.6 45.1 %collective-permute-start = (bf16[4,16,128,128]{3,2,1,0:T(8,128)(2,1)}, bf16[4,16,128,128]{3,2,1,0:T(8,128)(2,1)S(1)}, u32[]{:S(2)}, u32[]{:S(2)}) collective-permute-start(bf16[4,16,128,128]{3,2,1,0:T(8,128)(2,1)} %bitcast.13), channel_id=1, source_target_pairs={{0,32},{32,64},{64,96},{96,128},{128,160},{160,192},{192,224},{1,3... | collective-permute-start | bytes 6291464 | tf_op jit(solution)/shard_map/ppermute | solution.py:239
  3.3 25.0 %collective-permute-start.1 = (f32[2,4,128]{2,1,0:T(4,128)S(1)}, f32[2,4,128]{2,1,0:T(4,128)S(1)}, u32[]{:S(2)}, u32[]{:S(2)}) collective-permute-start(f32[2,4,128]{2,1,0:T(4,128)S(1)} %pad_maximum_fusion), channel_id=1, source_target_pairs={{0,32},{32,64},{64,96},{96,128},{128,160},{160,192},{192,224},{1,3... | collective-permute-start | bytes 12296 | tf_op jit(solution)/shard_map/ppermute | solution.py:239
  28.2 4.9 %collective-permute-start.2 = (f32[2,4,128]{2,1,0:T(4,128)S(1)}, f32[2,4,128]{2,1,0:T(4,128)S(1)}, u32[]{:S(2)}, u32[]{:S(2)}) collective-permute-start(f32[2,4,128]{2,1,0:T(4,128)S(1)} %collective-permute-done.1), channel_id=1, source_target_pairs={{0,32},{32,64},{64,96},{96,128},{128,160},{160,192},{192,224},{1,3... | collective-permute-start | bytes 12296 | tf_op jit(solution)/shard_map/ppermute | solution.py:239
  33.2 5.5 %collective-permute-start.3 = (f32[2,4,128]{2,1,0:T(4,128)S(1)}, f32[2,4,128]{2,1,0:T(4,128)S(1)}, u32[]{:S(2)}, u32[]{:S(2)}) collective-permute-start(f32[2,4,128]{2,1,0:T(4,128)S(1)} %pad_maximum_fusion.1), channel_id=1, source_target_pairs={{0,64},{32,96},{64,128},{96,160},{128,192},{160,224},{1,65},{33,97... | collective-permute-start | bytes 12296 | tf_op jit(solution)/shard_map/ppermute | solution.py:239
  38.7 7.0 %collective-permute-start.4 = (f32[2,4,128]{2,1,0:T(4,128)S(1)}, f32[2,4,128]{2,1,0:T(4,128)S(1)}, u32[]{:S(2)}, u32[]{:S(2)}) collective-permute-start(f32[2,4,128]{2,1,0:T(4,128)S(1)} %pad_maximum_fusion.2), channel_id=1, source_target_pairs={{0,128},{32,160},{64,192},{96,224},{1,129},{33,161},{65,193},{97,2... | collective-permute-start | bytes 12296 | tf_op jit(solution)/shard_map/ppermute | solution.py:239
  45.7 1.6 %copy-start = (bf16[1,4,16,128,128]{4,3,2,1,0:T(8,128)(2,1)S(1)}, bf16[1,4,16,128,128]{4,3,2,1,0:T(8,128)(2,1)}, u32[]{:S(2)}) copy-start(bf16[1,4,16,128,128]{4,3,2,1,0:T(8,128)(2,1)} %param.12) | copy-start | bytes 6291460
  47.3 1.6 %copy-start.1 = (bf16[1,4,16,128,128]{4,3,2,1,0:T(8,128)(2,1)S(1)}, bf16[1,4,16,128,128]{4,3,2,1,0:T(8,128)(2,1)}, u32[]{:S(2)}) copy-start(bf16[1,4,16,128,128]{4,3,2,1,0:T(8,128)(2,1)} %param.13) | copy-start | bytes 6291460
  48.9 1.0 copy-start.2
  49.9 1.0 copy-start.8
  51.0 0.9 copy-start.9
  51.9 0.8 copy-start.10
  52.7 0.8 copy-start.11
  53.5 48.0 %copy-start.3 = (bf16[1,4,128,4,128]{4,3,2,1,0:T(4,128)(2,1)S(1)}, bf16[1,4,128,4,128]{4,3,2,1,0:T(4,128)(2,1)}, u32[]{:S(2)}) copy-start(bf16[1,4,128,4,128]{4,3,2,1,0:T(4,128)(2,1)} %param.11) | copy-start | bytes 1572868
  60.6 1.0 copy-start.4
  61.6 1.0 copy-start.6
  62.6 38.9 %all-to-all-start = ((f32[32,1,128]{2,1,0:T(1,128)}), f32[32,1,128]{2,1,0:T(1,128)S(1)}, u32[]{:S(2)}, u32[]{:S(2)}) async-start(f32[32,1,128]{2,1,0:T(1,128)} %bitcast.6), calls=%async_computation | async-start | bytes 32768 | tf_op jit(solution)/shard_map/all_to_all | solution.py:294
  101.5 1.2 %copy-start.5 = (f32[4,512,128]{2,1,0:T(8,128)S(1)}, f32[4,512,128]{2,1,0:T(8,128)}, u32[]{:S(2)}) copy-start(f32[4,512,128]{2,1,0:T(8,128)} %copy-done.4) | copy-start | bytes 3145732
  102.7 1.2 %copy-start.7 = (f32[4,512,128]{2,1,0:T(8,128)S(1)}, f32[4,512,128]{2,1,0:T(8,128)}, u32[]{:S(2)}) copy-start(f32[4,512,128]{2,1,0:T(8,128)} %copy-done.6) | copy-start | bytes 3145732
where the time goes:
time: 107 us; the launch traced here: 106 us
  waiting for transfers between devices  43.3 us (40%)
  starting transfers between devices  37.6 us (35%)
  local copies, waits for them, and re-layouts  13.8 us (13%)
  Pallas kernels  9.26 us (9%)
  between operations  1.35 us (1%)
    ppermute x5, waiting for transfers between devices, from_behind(): return lax.ppermute(shard, axis, [(i, i + by) for i in range(length - by)])  34.4 us
    all_to_all x1, starting transfers between devices, body(): lax.all_to_all(sums.reshape(sectors, 1, BLK), 'sector', 0, 0)  29.3 us
    unnamed x24, local copies, waits for them, and re-layouts  12.2 us
    all_to_all x1, waiting for transfers between devices, body(): lax.all_to_all(sums.reshape(sectors, 1, BLK), 'sector', 0, 0)  8.95 us
    ppermute x5, starting transfers between devices, from_behind(): return lax.ppermute(shard, axis, [(i, i + by) for i in range(length - by)])  8.32 us
    pallas_call x1, Pallas kernels, body(): pl.pallas_call(krylov_kernel, grid=(slots,), in_specs=[smem, smem, block(...  7.15 us
  transfers between devices with their start and end apart: 6, of which 5 were waited for; matrix products, arithmetic and copies ran while one was open for 2% of the time, Pallas kernels for 0%

commit v1 on v0

v1 whole, which is shorter than its diff:
```python
import functools
import math

import jax
import jax.numpy as jnp
import numpy as np
from jax import lax
from jax.experimental import pallas as pl
from jax.experimental.pallas import tpu as pltpu
from jax.sharding import PartitionSpec as P

DAV = 2
EPS = 1e-06
BLK = 128
PHYS = 4
CHAN = 16
ROWS = BLK * PHYS
GROUP = 4
VMEM_LIMIT = 56 << 20
GROUPED = 2
STRIDE = 8

(NORM, SHIFT, RES, BACK, DIAG, DEEP, ON_F, ON_R, ON_D) = range(9)


def constants():
    lanes = np.zeros((4 * BLK, 4 * BLK), np.float32)
    for u in range(4):
        for a in range(BLK):
            lanes[u * BLK + a, (a // GROUP) * 16 + u * GROUP + a % GROUP] = 1.0
    rows = np.zeros((256, 64), np.float32)
    cols = np.zeros((64, 256), np.float32)
    same = np.zeros((256, 256), np.float32)
    for s in range(PHYS):
        for u in range(CHAN):
            for g in range(GROUP):
                rows[s * 64 + u * GROUP + g, u * PHYS + s] = 1.0
    for t in range(PHYS):
        for w in range(CHAN):
            for g in range(GROUP):
                cols[t * CHAN + w, w * 16 + g * PHYS + t] = 1.0
    index = np.arange(256)
    same[:, :] = (index[:, None] % GROUP) == ((index[None, :] // PHYS) % GROUP)
    return [jnp.asarray(m, jnp.bfloat16) for m in (lanes, rows, cols, same)]


def matmul(x, y):
    return jnp.dot(x, y, preferred_element_type=jnp.float32)


def total(x):
    return jnp.sum(jnp.sum(x, axis=0, keepdims=True), axis=1, keepdims=True)


def ratio(top, bottom):
    return jnp.where(bottom > 0.0, top / jnp.where(bottom > 0.0, bottom, 1.0), 0.0)


def operator_kernel(mpo_ref, rows_ref, cols_ref, same_ref, operator_ref):
    wide = matmul(rows_ref[...], mpo_ref[...]).astype(jnp.bfloat16)
    wide = matmul(wide, cols_ref[...]).astype(jnp.bfloat16)
    operator_ref[...] = wide * same_ref[...]


def krylov_kernel(
    base, live_ref, region_ref, before_ref, offset_ref, operator_ref,
    start_hbm, own_hbm, left_hbm, right_hbm, lanes_hbm,
    sums_ref, res_hbm, deep_hbm,
    start_ref, left_ref, right_ref, lanes_ref, res_ref, deep_ref,
    left_lanes, first_half, second_half, spread, shift, sems,
):
    group = range(start_ref.shape[0])

    def operate_right(i, vector):
        for pair in range(CHAN // 2):
            right = jnp.concatenate([right_ref[i, 2 * pair], right_ref[i, 2 * pair + 1]], axis=1)
            made = matmul(vector, right).astype(jnp.bfloat16)
            for j in range(2):
                w = 2 * pair + j
                for half in range(2):
                    part = made[half * 256:(half + 1) * 256, j * BLK:(j + 1) * BLK]
                    first_half[i, :, w * 16:(w + 1) * 16, half * BLK:(half + 1) * BLK] = part.reshape(16, 16, BLK)
        for g in range(16):
            made = matmul(operator_ref[...], first_half[i, g]).astype(jnp.bfloat16)
            for half in range(2):
                for s in range(PHYS):
                    for ug in range(4):
                        at = ug * 512 + (half * 16 + g) * 16
                        second_half[i, at:at + 16, s * BLK:(s + 1) * BLK] = made[
                            s * 64 + ug * 16:s * 64 + ug * 16 + 16, half * BLK:(half + 1) * BLK]

    def operate_left(i):
        made = matmul(left_lanes[i], second_half[i])
        for s in range(PHYS):
            spread[i, pl.ds(s, BLK, stride=PHYS), :] = made[:, s * BLK:(s + 1) * BLK]
        return spread[i]

    def order_lanes(i):
        for ug in range(4):
            four = jnp.concatenate([left_ref[i, 4 * ug + j] for j in range(4)], axis=1)
            left_lanes[i, :, ug * 512:(ug + 1) * 512] = matmul(four, lanes_ref[...]).astype(jnp.bfloat16)

    live = live_ref[0, 0]
    outer = region_ref[0] == 0
    lane = lax.broadcasted_iota(jnp.int32, (1, BLK), 1)

    @pl.when(base < live)
    def _():
        start_in = pltpu.make_async_copy(start_hbm.at[pl.ds(base, len(group))], start_ref, sems.at[0])
        right_in = [
            pltpu.make_async_copy(right_hbm.at[base + i], right_ref.at[i], sems.at[6 + i]) for i in group
        ]
        lanes_in = pltpu.make_async_copy(lanes_hbm, lanes_ref, sems.at[2])
        left_in = pltpu.make_async_copy(left_hbm, left_ref, sems.at[3])
        start_in.start()
        right_in[0].start()
        lanes_in.start()

        @pl.when(outer)
        def _():
            pltpu.make_async_copy(own_hbm.at[pl.ds(base, len(group))], left_ref, sems.at[3]).start()

        @pl.when(jnp.logical_not(outer))
        def _():
            left_in.start()

        for copy in right_in[1:]:
            copy.start()
        sums = before_ref[...]

        def note(sums, i, quantity, value):
            slot = base + i
            return sums + jnp.where(jnp.logical_and(lane == quantity * STRIDE + slot, slot < live), value, 0.0)

        for i in group:
            column = jnp.broadcast_to(offset_ref[base + i:base + i + 1, :], (BLK, BLK)).T
            for s in range(PHYS):
                shift[i, pl.ds(s, BLK, stride=PHYS), :] = column
        start_in.wait()
        for i in group:
            right_in[i].wait()
        lanes_in.wait()
        left_in.wait()
        res_out = pltpu.make_async_copy(res_ref, res_hbm, sems.at[4])
        deep_out = pltpu.make_async_copy(deep_ref, deep_hbm, sems.at[5])
        norm, res_norm = {}, {}

        for i in group:
            operate_right(i, start_ref[i])
            order_lanes(i)
        for i in group:
            first = start_ref[i].astype(jnp.float32)
            image = operate_left(i) + shift[i] * first
            norm[i] = total(first * first)
            quotient = ratio(total(first * image), norm[i])
            res = image - quotient * first
            res_ref[i] = res
            res_norm[i] = total(res * res)
            sums = note(note(note(sums, i, NORM, norm[i]), i, SHIFT, quotient), i, RES, res_norm[i])

        for i in group:
            operate_right(i, res_ref[i].astype(jnp.bfloat16))
        for i in group:
            res = res_ref[i]
            first = start_ref[i].astype(jnp.float32)
            image = operate_left(i) + shift[i] * res.astype(jnp.bfloat16).astype(jnp.float32)
            back = ratio(total(first * image), norm[i])
            diag = ratio(total(res * image), res_norm[i])
            deep = image - back * first - diag * res
            deep_ref[i] = deep
            sums = note(note(note(sums, i, BACK, back), i, DIAG, diag), i, DEEP, total(deep * deep))

        for i in group:
            operate_right(i, deep_ref[i].astype(jnp.bfloat16))
        for i in group:
            deep = deep_ref[i]
            image = operate_left(i) + shift[i] * deep.astype(jnp.bfloat16).astype(jnp.float32)
            sums = note(sums, i, ON_F, total(start_ref[i].astype(jnp.float32) * image))
            sums = note(sums, i, ON_R, total(res_ref[i] * image))
            sums = note(sums, i, ON_D, total(deep * image))
        res_out.start()
        deep_out.start()
        sums_ref[...] = jnp.broadcast_to(sums, sums_ref.shape)
        res_out.wait()
        deep_out.wait()

    @pl.when(base >= live)
    def _():
        sums_ref[...] = jnp.broadcast_to(before_ref[...], sums_ref.shape)


def rotate_kernel(
    scale, slots, sectors, live_ref, all_ref, own_ref, start_hbm, *refs
):
    groups = slots // GROUPED
    res_hbm, deep_hbm = refs[:groups], refs[groups:2 * groups]
    state_hbm, density_hbm, energy_ref = refs[2 * groups:2 * groups + 3]
    start_ref, res_ref, deep_ref, state_ref, density_ref, spread, sems = refs[2 * groups + 3:]
    live = live_ref[0, 0]

    def coming(slot):
        return (
            pltpu.make_async_copy(start_hbm.at[slot], start_ref.at[slot], sems.at[0, slot]),
            pltpu.make_async_copy(res_hbm[slot // GROUPED].at[slot % GROUPED], res_ref.at[slot], sems.at[1, slot]),
            pltpu.make_async_copy(deep_hbm[slot // GROUPED].at[slot % GROUPED], deep_ref.at[slot], sems.at[2, slot]),
        )

    def going(slot):
        return (
            pltpu.make_async_copy(state_ref.at[slot], state_hbm.at[slot], sems.at[3, slot]),
            pltpu.make_async_copy(density_ref.at[slot], density_hbm.at[slot], sems.at[4, slot]),
        )

    for slot in range(slots):

        @pl.when(slot < live)
        def _():
            for copy in coming(slot):
                copy.start()

        @pl.when(slot >= live)
        def _():
            state_ref[slot] = jnp.zeros(state_ref.shape[1:], state_ref.dtype)
            density_ref[slot] = jnp.zeros(density_ref.shape[1:], density_ref.dtype)
            for copy in going(slot):
                copy.start()

    table = jnp.concatenate([all_ref[...], own_ref[0:8, :]], axis=0)
    shape = (sectors + 8, BLK)
    row = lax.broadcasted_iota(jnp.int32, shape, 0)
    lane = lax.broadcasted_iota(jnp.int32, shape, 1)
    counted = jnp.logical_and(row < sectors, lane < STRIDE)

    def pick(quantity):
        return table if quantity == 0 else pltpu.roll(table, BLK - quantity * STRIDE, 1)

    def region_sum(x):
        return total(jnp.where(counted, x, 0.0))

    norm, shift, res_norm, back, diag, deep_norm, on_f, on_r, on_d = [pick(k) for k in range(9)]
    grams = (norm, res_norm, deep_norm)
    zero = jnp.zeros(shape, jnp.float32)

    def inner(x, y):
        made = x[0] * y[0] * grams[0]
        for k in (1, 2):
            made = made + x[k] * y[k] * grams[k]
        if len(y) > 3:
            made = made + y[3] * (x[0] * on_f + x[1] * on_r + x[2] * on_d)
        return region_sum(made)

    inverse = lax.rsqrt(region_sum(norm) + EPS)
    current = (zero + inverse, zero, zero)
    applied = (inverse * shift, zero + inverse, zero)
    for iteration in range(DAV):
        quotient = inner(current, applied)
        residual = tuple(x - quotient * y for x, y in zip(applied, current))
        resid_sq = inner(residual, residual)
        factor = lax.rsqrt(resid_sq + EPS)
        search = tuple(factor * x for x in residual)
        image = (search[0] * shift + search[1] * back, search[0] + search[1] * diag, search[1])
        if iteration == 1:
            image = image + (search[2],)
        curvature = inner(search, image)
        opposite = -2.0 * resid_sq * factor
        adjacent = curvature - quotient
        largest = jnp.maximum(jnp.abs(opposite), jnp.abs(adjacent))
        flat = largest == 0.0
        largest = jnp.where(flat, 1.0, largest)
        opposite = opposite / largest
        adjacent = jnp.where(flat, 1.0, adjacent / largest)
        length = jnp.sqrt(opposite * opposite + adjacent * adjacent)
        double_cos = jnp.abs(adjacent) / length
        double_sin = jnp.abs(opposite) / length
        large = jnp.sqrt(0.5 + 0.5 * double_cos)
        small = double_sin / (2.0 * large)
        ahead = adjacent >= 0.0
        cos_part = jnp.where(ahead, large, small)
        sin_part = -jnp.where(ahead, small, large)
        current = tuple(cos_part * x + sin_part * y for x, y in zip(current, search))
        turned = tuple(cos_part * x + sin_part * y for x, y in zip(applied, image))
        applied = turned + tuple(sin_part * y for y in image[3:])
    energy_ref[...] = jnp.broadcast_to(inner(current, applied), energy_ref.shape)
    mine = [scale * x[sectors:sectors + 1, :] for x in current]
    for slot in range(slots):

        @pl.when(slot < live)
        def _():
            for copy in coming(slot):
                copy.wait()
            on_first, on_res, on_deep = [x[:, slot:slot + 1] for x in mine]
            state = on_first * start_ref[slot].astype(jnp.float32)
            state = state + on_res * res_ref[slot] + on_deep * deep_ref[slot]
            state = state.astype(jnp.bfloat16)
            state_ref[slot] = state
            spread[slot] = state.astype(jnp.float32)
            wide = jnp.concatenate(
                [spread[slot, pl.ds(s, BLK, stride=PHYS), :] for s in range(PHYS)], axis=1
            ).astype(jnp.bfloat16)
            product = lax.dot_general(
                wide, wide, (((1,), (1,)), ((), ())), preferred_element_type=jnp.float32
            )
            density_ref[slot] = product * (1.0 / ROWS)
            for copy in going(slot):
                copy.start()

    for slot in range(slots):
        for copy in going(slot):
            copy.wait()


def from_behind(shard, axis, by):
    length = lax.axis_size(axis)
    return lax.ppermute(shard, axis, [(i, i + by) for i in range(length - by)])


def entering(decay, terms, axis):
    slots = decay.shape[0]
    own = jnp.concatenate([decay, terms], axis=0)
    other = lax.ppermute(own, axis, [(i, i ^ 1) for i in range(lax.axis_size(axis))])
    second = lax.axis_index(axis) % 2 == 1
    early, late = jnp.where(second, other, own), jnp.where(second, own, other)
    pair = jnp.concatenate(
        [early[:slots] * late[:slots], late[:slots] * early[slots:] + late[slots:]], axis=0
    )
    total = jnp.zeros_like(terms)
    for by in (6, 4, 2):
        earlier = from_behind(pair, axis, by)
        total = earlier[:slots] * total + earlier[slots:]
    return jnp.where(second, early[:slots] * total + early[slots:], total)


def body(start_state, left_env, right_env, mpo_tensor, decay, energy_terms, live_count):
    slots = start_state.shape[1]
    sectors = lax.axis_size("sector")
    start = start_state.reshape(slots, ROWS, BLK)
    offsets = entering(decay[0], energy_terms[0], "region")
    arrived = [from_behind(left_env[0, at:at + GROUPED], "region", 1) for at in range(0, slots, GROUPED)]
    region = lax.axis_index("region").reshape(1).astype(jnp.int32)
    mpo = mpo_tensor.reshape(CHAN * PHYS, PHYS * CHAN)
    lanes, rows, cols, same = constants()

    smem = pl.BlockSpec(memory_space=pltpu.SMEM)
    vmem = pl.BlockSpec(memory_space=pltpu.VMEM)
    hbm = pl.BlockSpec(memory_space=pl.ANY)
    vectors = jax.ShapeDtypeStruct((GROUPED, ROWS, BLK), jnp.float32)
    operator = pl.pallas_call(
        operator_kernel,
        in_specs=[vmem] * 4,
        out_specs=vmem,
        out_shape=jax.ShapeDtypeStruct((256, 256), jnp.bfloat16),
        name="operator",
    )(mpo, rows, cols, same)
    sums = jnp.zeros((1, BLK), jnp.float32)
    res, deep = [], []
    for base in range(0, slots, GROUPED):
        copies = sectors if base + GROUPED == slots else 1
        sums, res_one, deep_one = pl.pallas_call(
            functools.partial(krylov_kernel, base),
            in_specs=[smem, smem, vmem, vmem, vmem, hbm, hbm, hbm, hbm, hbm],
            out_specs=[vmem, hbm, hbm],
            out_shape=[jax.ShapeDtypeStruct((copies, BLK), jnp.float32), vectors, vectors],
            scratch_shapes=[
                pltpu.VMEM((GROUPED, ROWS, BLK), jnp.bfloat16),
                pltpu.VMEM((GROUPED, CHAN, BLK, BLK), jnp.bfloat16),
                pltpu.VMEM((GROUPED, CHAN, BLK, BLK), jnp.bfloat16),
                pltpu.VMEM((4 * BLK, 4 * BLK), jnp.bfloat16),
                pltpu.VMEM((GROUPED, ROWS, BLK), jnp.float32),
                pltpu.VMEM((GROUPED, ROWS, BLK), jnp.float32),
                pltpu.VMEM((GROUPED, BLK, CHAN * BLK), jnp.bfloat16),
                pltpu.VMEM((GROUPED, 16, 256, 256), jnp.bfloat16),
                pltpu.VMEM((GROUPED, CHAN * BLK, ROWS), jnp.bfloat16),
                pltpu.VMEM((GROUPED, ROWS, BLK), jnp.float32),
                pltpu.VMEM((GROUPED, ROWS, BLK), jnp.float32),
                pltpu.SemaphoreType.DMA((6 + GROUPED,)),
            ],
            compiler_params=pltpu.CompilerParams(vmem_limit_bytes=VMEM_LIMIT),
            cost_estimate=pl.CostEstimate(flops=10**10, bytes_accessed=1 << 22, transcendentals=0),
            name="krylov",
        )(
            live_count, region, sums, offsets, operator,
            start, left_env[0], arrived[base // GROUPED], right_env[0], lanes,
        )
        res.append(res_one)
        deep.append(deep_one)
    every = lax.all_to_all(sums.reshape(sectors, 1, BLK), "sector", 0, 0).reshape(sectors, BLK)
    state, density, energy = pl.pallas_call(
        functools.partial(rotate_kernel, math.sqrt(slots * sectors * ROWS * BLK), slots, sectors),
        in_specs=[smem, vmem, vmem] + [hbm] * (1 + 2 * (slots // GROUPED)),
        out_specs=[hbm, hbm, vmem],
        out_shape=[
            jax.ShapeDtypeStruct((slots, ROWS, BLK), jnp.bfloat16),
            jax.ShapeDtypeStruct((slots, BLK, BLK), jnp.float32),
            jax.ShapeDtypeStruct((1, 1), jnp.float32),
        ],
        scratch_shapes=[
            pltpu.VMEM((slots, ROWS, BLK), jnp.bfloat16),
            pltpu.VMEM((slots, ROWS, BLK), jnp.float32),
            pltpu.VMEM((slots, ROWS, BLK), jnp.float32),
            pltpu.VMEM((slots, ROWS, BLK), jnp.bfloat16),
            pltpu.VMEM((slots, BLK, BLK), jnp.float32),
            pltpu.VMEM((slots, ROWS, BLK), jnp.float32),
            pltpu.SemaphoreType.DMA((5, slots)),
        ],
        compiler_params=pltpu.CompilerParams(vmem_limit_bytes=VMEM_LIMIT),
        name="rotate",
    )(live_count, every, sums, start, *res, *deep)
    return (state.reshape(start_state.shape), density[None], energy.reshape(1))


def solution(mesh):
    in_specs = (
        P("region", "sector", None, None, None),
        P("region", "sector", None, None, None),
        P("region", "sector", None, None, None),
        P(),
        P("region", "sector", None),
        P("region", "sector", None),
        P("region", "sector"),
    )
    out_specs = (
        P("region", "sector", None, None, None),
        P("region", "sector", None, None),
        P("region"),
    )
    return jax.shard_map(body, mesh=mesh, in_specs=in_specs, out_specs=out_specs, check_vma=False)
```

time: 107 us -> 73.9 us (0.69)
  the two profiles are of different devices: /device:TPU:6 before, /device:TPU:1 now
where the time goes in v1:
time: 73.9 us; the launch traced here: 73.1 us
  blocking collectives  31 us (42%)
  Pallas kernels  20.6 us (28%)
  starting transfers between devices  14 us (19%)
  local copies, waits for them, and re-layouts  3.43 us (5%)
  waiting for transfers between devices  1.96 us (3%)
  between operations  1.58 us (2%)
    all_to_all x1, blocking collectives, body(): lax.all_to_all(sums.reshape(sectors, 1, BLK), 'sector', 0, 0)  31 us
    pallas_call x2, Pallas kernels, body(): pl.pallas_call(functools.partial(krylov_kernel, base), in_specs=[smem, sm...  14.7 us
    ppermute x5, starting transfers between devices, from_behind(): return lax.ppermute(shard, axis, [(i, i + by) for i in range(length - by)])  13.8 us
    pallas_call x1, Pallas kernels, body(): pl.pallas_call(functools.partial(rotate_kernel, math.sqrt(slots * sectors...  3.91 us
    ppermute x1, waiting for transfers between devices, entering(): lax.ppermute(own, axis, [(i, i ^ 1) for i in range(lax.axis_size(axis))])  1.95 us
    pallas_call x1, Pallas kernels, body(): pl.pallas_call(operator_kernel, in_specs=[vmem] * 4, out_specs=vmem, out_...  1.94 us
    squeeze x1, local copies, waits for them, and re-layouts, body(): left_env[0, at:at + GROUPED]  1.71 us
  transfers between devices with their start and end apart: 6, of which 1 were waited for; matrix products, arithmetic and copies ran while one was open for 3% of the time, Pallas kernels for 21%

profile of v1, /device:TPU:1, one launch (start us, length us, event | category | flops | bytes accessed | tf_op | source)
XLA Modules:
  0.0 73.1 jit_solution(16325405154183990702)
XLA Ops:
  0.6 0.0 copy-start.1
  0.6 0.0 copy-start.2
  0.7 0.0 copy-start
  0.7 1.7 %slice_bitcast_fusion = (bf16[2,16,128,128]{3,2,1,0:T(8,128)(2,1)S(1)}, bf16[2,16,128,128]{3,2,1,0:T(8,128)(2,1)S(1)}) fusion(bf16[1,4,16,128,128]{4,3,2,1,0:T(8,128)(2,1)} %param.12), kind=kLoop, calls=%fused_computation | loop fusion | bytes 4194304 | tf_op jit(solution)/shard_map/squeeze | solution.py:338
  2.4 4.5 %collective-permute-start.4 = (bf16[2,16,128,128]{3,2,1,0:T(8,128)(2,1)S(1)}, bf16[2,16,128,128]{3,2,1,0:T(8,128)(2,1)S(1)}, u32[]{:S(2)}, u32[]{:S(2)}) collective-permute-start(bf16[2,16,128,128]{3,2,1,0:T(8,128)(2,1)S(1)} %get-tuple-element.22), channel_id=1, source_target_pairs={{0,32},{32,64},{64,96},{96,128},{128,160},{160,192},{192,224},{1,3... | collective-permute-start | bytes 3145736 | tf_op jit(solution)/shard_map/ppermute | solution.py:314
  6.9 0.0 copy-done.1
  6.9 0.0 copy-done.2
  6.9 0.2 collective-permute-start
  7.1 1.9 %collective-permute-done = f32[8,128]{1,0:T(8,128)S(1)} collective-permute-done((f32[8,128]{1,0:T(8,128)S(1)}, f32[8,128]{1,0:T(8,128)S(1)}, u32[]{:S(2)}, u32[]{:S(2)}) %collective-permute-start) | collective-permute-done | bytes 4128 | tf_op jit(solution)/shard_map/ppermute | solution.py:320
  9.1 3.3 %collective-permute-start.3 = (f32[8,128]{1,0:T(8,128)S(1)}, f32[8,128]{1,0:T(8,128)S(1)}, u32[]{:S(2)}, u32[]{:S(2)}) collective-permute-start(f32[8,128]{1,0:T(8,128)S(1)} %pad_maximum_fusion.1), channel_id=1, source_target_pairs={{0,192},{32,224},{1,193},{33,225},{2,194},{34,226},{3,195},{35,227... | collective-permute-start | bytes 12296 | tf_op jit(solution)/shard_map/ppermute | solution.py:314
  12.4 1.3 %collective-permute-start.2 = (f32[8,128]{1,0:T(8,128)S(1)}, f32[8,128]{1,0:T(8,128)S(1)}, u32[]{:S(2)}, u32[]{:S(2)}) collective-permute-start(f32[8,128]{1,0:T(8,128)S(1)} %pad_maximum_fusion.1), channel_id=1, source_target_pairs={{0,128},{32,160},{64,192},{96,224},{1,129},{33,161},{65,193},{97,2... | collective-permute-start | bytes 12296 | tf_op jit(solution)/shard_map/ppermute | solution.py:314
  13.7 2.5 %collective-permute-start.1 = (f32[8,128]{1,0:T(8,128)S(1)}, f32[8,128]{1,0:T(8,128)S(1)}, u32[]{:S(2)}, u32[]{:S(2)}) collective-permute-start(f32[8,128]{1,0:T(8,128)S(1)} %pad_maximum_fusion.1), channel_id=1, source_target_pairs={{0,64},{32,96},{64,128},{96,160},{128,192},{160,224},{1,65},{33,97... | collective-permute-start | bytes 12296 | tf_op jit(solution)/shard_map/ppermute | solution.py:314
  16.2 2.2 %collective-permute-start.5 = (bf16[2,16,128,128]{3,2,1,0:T(8,128)(2,1)S(1)}, bf16[2,16,128,128]{3,2,1,0:T(8,128)(2,1)}, u32[]{:S(2)}, u32[]{:S(2)}) collective-permute-start(bf16[2,16,128,128]{3,2,1,0:T(8,128)(2,1)S(1)} %get-tuple-element.21), channel_id=1, source_target_pairs={{0,32},{32,64},{64,96},{96,128},{128,160},{160,192},{192,224},{1,3... | collective-permute-start | bytes 3145736 | tf_op jit(solution)/shard_map/ppermute | solution.py:314
  19.1 0.0 copy-done
  19.1 0.7 reshape.28.mpo_ref
  19.8 1.9 %operator.1.operator_ref = bf16[256,256]{1,0:T(8,128)(2,1)} custom-call(bf16[64,64]{1,0:T(8,128)(2,1)} %reshape.28.mpo_ref, bf16[256,64]{1,0:T(8,128)(2,1)} %constant.32.clone.rows_ref, bf16[64,256]{1,0:T(8,128)(2,1)} %constant.33.clone.cols_ref, bf16[256,256]{1,0:T(8,128)(2,1)} %constant.34.clone.same_ref), custom_call_target="tpu_custom_call" | custom-call | tf_op jit(solution)/shard_map/operator/pallas_call | solution.py:347
  21.7 0.0 collective-permute-done.3
  21.7 0.0 collective-permute-done.2
  21.7 0.0 collective-permute-done.1
  21.7 0.6 add_select_fusion.offset_ref
  22.3 0.0 collective-permute-done.4.left_hbm
  22.3 0.0 copy-start.3
  22.3 0.5 broadcast_in_dim.9.before_ref
  22.9 0.4 copy-done.3
  23.3 13.1 %krylov.2 = (f32[1,128]{1,0:T(1,128)}, f32[2,512,128]{2,1,0:T(8,128)}, f32[2,512,128]{2,1,0:T(8,128)}) custom-call(s32[1,1]{1,0:T(1,128)S(6)} %copy.15.live_ref, s32[1]{0:T(128)} %bitcast.region_ref, f32[1,128]{1,0:T(1,128)} %broadcast_in_dim.9.before_ref, f32[4,128]{1,0:T(4,128)} %add_select_fusion.offset_ref, bf16[256,256]{1,0:T(8,128)(2,1)} %operator.1.operator_ref, ...), custom_call_target="tpu_custom_call" | custom-call | flops 10000000000 | bytes 4194304 | tf_op jit(solution)/shard_map/krylov/pallas_call | solution.py:358
  36.5 0.0 collective-permute-done.5.left_hbm
  36.5 1.6 %krylov.3 = (f32[32,128]{1,0:T(8,128)}, f32[2,512,128]{2,1,0:T(8,128)}, f32[2,512,128]{2,1,0:T(8,128)}) custom-call(s32[1,1]{1,0:T(1,128)S(6)} %copy.15.live_ref, s32[1]{0:T(128)} %bitcast.region_ref, f32[1,128]{1,0:T(1,128)} %get-tuple-element.12.before_ref, f32[4,128]{1,0:T(4,128)} %add_select_fusion.offset_ref, bf16[256,256]{1,0:T(8,128)(2,1)} %operator.1.operator_ref, ...), custom_call_target="tpu_custom_call" | custom-call | flops 10000000000 | bytes 4194304 | tf_op jit(solution)/shard_map/krylov/pallas_call | solution.py:358
  38.1 31.0 %all_to_all.5 = f32[32,1,128]{2,1,0:T(1,128)} all-to-all(f32[32,1,128]{2,1,0:T(1,128)} %bitcast.22), channel_id=1, replica_groups=mesh['region'=8,'sector'=32] {'sector'}, dimensions={0} | all-to-all | bytes 32768 | tf_op jit(solution)/shard_map/all_to_all | solution.py:386
  69.1 3.9 %rotate.1 = (bf16[4,512,128]{2,1,0:T(8,128)(2,1)}, f32[4,128,128]{2,1,0:T(8,128)}, f32[1,1]{1,0:T(1,128)}) custom-call(s32[1,1]{1,0:T(1,128)S(6)} %copy.15.live_ref, f32[32,128]{1,0:T(8,128)} %bitcast.23, f32[32,128]{1,0:T(8,128)} %get-tuple-element.13.own_ref, bf16[4,512,128]{2,1,0:T(8,128)(2,1)} %bitcast.21, f32[2,512,128]{2,1,0:T(8,128)} %get-tuple-element.14.refs_0_, ...), custom_call_target="tpu_custom_call" | custom-call | tf_op jit(solution)/shard_map/rotate/pallas_call | solution.py:387
  (4 shorter events, 0.0 us)
Async XLA Ops:
  0.6 6.3 %copy-start.1 = (f32[1,4,128]{2,1,0:T(4,128)S(1)}, f32[1,4,128]{2,1,0:T(4,128)}, u32[]{:S(2)}) copy-start(f32[1,4,128]{2,1,0:T(4,128)} %param.16) | copy-start | bytes 6148
  0.6 6.3 %copy-start.2 = (f32[1,4,128]{2,1,0:T(4,128)S(1)}, f32[1,4,128]{2,1,0:T(4,128)}, u32[]{:S(2)}) copy-start(f32[1,4,128]{2,1,0:T(4,128)} %param.15) | copy-start | bytes 6148
  0.7 18.4 %copy-start = (bf16[16,4,4,16]{3,2,1,0:T(4,128)(2,1)S(1)}, bf16[16,4,4,16]{3,2,1,0:T(4,128)(2,1)}, u32[]{:S(2)}) copy-start(bf16[16,4,4,16]{3,2,1,0:T(4,128)(2,1)} %param.14) | copy-start | bytes 24580
  2.4 20.0 %collective-permute-start.4 = (bf16[2,16,128,128]{3,2,1,0:T(8,128)(2,1)S(1)}, bf16[2,16,128,128]{3,2,1,0:T(8,128)(2,1)S(1)}, u32[]{:S(2)}, u32[]{:S(2)}) collective-permute-start(bf16[2,16,128,128]{3,2,1,0:T(8,128)(2,1)S(1)} %get-tuple-element.22), channel_id=1, source_target_pairs={{0,32},{32,64},{64,96},{96,128},{128,160},{160,192},{192,224},{1,3... | collective-permute-start | bytes 3145736 | tf_op jit(solution)/shard_map/ppermute | solution.py:314
  6.9 2.1 %collective-permute-start = (f32[8,128]{1,0:T(8,128)S(1)}, f32[8,128]{1,0:T(8,128)S(1)}, u32[]{:S(2)}, u32[]{:S(2)}) collective-permute-start(f32[8,128]{1,0:T(8,128)S(1)} %pad_maximum_fusion), channel_id=1, source_target_pairs={{0,32},{32,0},{64,96},{96,64},{128,160},{160,128},{192,224},{224,1... | collective-permute-start | bytes 12296 | tf_op jit(solution)/shard_map/ppermute | solution.py:320
  9.1 12.6 %collective-permute-start.3 = (f32[8,128]{1,0:T(8,128)S(1)}, f32[8,128]{1,0:T(8,128)S(1)}, u32[]{:S(2)}, u32[]{:S(2)}) collective-permute-start(f32[8,128]{1,0:T(8,128)S(1)} %pad_maximum_fusion.1), channel_id=1, source_target_pairs={{0,192},{32,224},{1,193},{33,225},{2,194},{34,226},{3,195},{35,227... | collective-permute-start | bytes 12296 | tf_op jit(solution)/shard_map/ppermute | solution.py:314
  12.4 9.4 %collective-permute-start.2 = (f32[8,128]{1,0:T(8,128)S(1)}, f32[8,128]{1,0:T(8,128)S(1)}, u32[]{:S(2)}, u32[]{:S(2)}) collective-permute-start(f32[8,128]{1,0:T(8,128)S(1)} %pad_maximum_fusion.1), channel_id=1, source_target_pairs={{0,128},{32,160},{64,192},{96,224},{1,129},{33,161},{65,193},{97,2... | collective-permute-start | bytes 12296 | tf_op jit(solution)/shard_map/ppermute | solution.py:314
  13.7 8.1 %collective-permute-start.1 = (f32[8,128]{1,0:T(8,128)S(1)}, f32[8,128]{1,0:T(8,128)S(1)}, u32[]{:S(2)}, u32[]{:S(2)}) collective-permute-start(f32[8,128]{1,0:T(8,128)S(1)} %pad_maximum_fusion.1), channel_id=1, source_target_pairs={{0,64},{32,96},{64,128},{96,160},{128,192},{160,224},{1,65},{33,97... | collective-permute-start | bytes 12296 | tf_op jit(solution)/shard_map/ppermute | solution.py:314
  16.2 20.3 %collective-permute-start.5 = (bf16[2,16,128,128]{3,2,1,0:T(8,128)(2,1)S(1)}, bf16[2,16,128,128]{3,2,1,0:T(8,128)(2,1)}, u32[]{:S(2)}, u32[]{:S(2)}) collective-permute-start(bf16[2,16,128,128]{3,2,1,0:T(8,128)(2,1)S(1)} %get-tuple-element.21), channel_id=1, source_target_pairs={{0,32},{32,64},{64,96},{96,128},{128,160},{160,192},{192,224},{1,3... | collective-permute-start | bytes 3145736 | tf_op jit(solution)/shard_map/ppermute | solution.py:314
  22.3 1.0 %copy-start.3 = (bf16[2,16,128,128]{3,2,1,0:T(8,128)(2,1)}, bf16[2,16,128,128]{3,2,1,0:T(8,128)(2,1)S(1)}, u32[]{:S(2)}) copy-start(bf16[2,16,128,128]{3,2,1,0:T(8,128)(2,1)S(1)} %collective-permute-done.4.left_hbm) | copy-start | bytes 3145732

commit v2 on v1

--- a/solution.py
+++ b/solution.py
@@ -56,19 +56,22 @@
     return jnp.where(bottom > 0.0, top / jnp.where(bottom > 0.0, bottom, 1.0), 0.0)
 
 
-def operator_kernel(mpo_ref, rows_ref, cols_ref, same_ref, operator_ref):
-    wide = matmul(rows_ref[...], mpo_ref[...]).astype(jnp.bfloat16)
-    wide = matmul(wide, cols_ref[...]).astype(jnp.bfloat16)
-    operator_ref[...] = wide * same_ref[...]
-
-
 def krylov_kernel(
-    base, live_ref, region_ref, before_ref, offset_ref, operator_ref,
-    start_hbm, own_hbm, left_hbm, right_hbm, lanes_hbm,
-    sums_ref, res_hbm, deep_hbm,
-    start_ref, left_ref, right_ref, lanes_ref, res_ref, deep_ref,
-    left_lanes, first_half, second_half, spread, shift, sems,
+    base, live_ref, region_ref, offset_hbm, start_hbm, own_hbm, left_hbm, right_hbm, lanes_hbm, *refs
 ):
+    head = base == 0
+    if head:
+        small_hbm, (sums_ref, res_hbm, deep_hbm, operator_hbm) = refs[:4], refs[4:8]
+        refs = refs[8:]
+    else:
+        small_hbm, (sums_ref, res_hbm, deep_hbm) = refs[:2], refs[2:5]
+        refs = refs[5:]
+    (
+        start_ref, left_ref, right_ref, lanes_ref, res_ref, deep_ref,
+        left_lanes, first_half, second_half, spread, shift, offset_ref, operator_ref, sems, *small,
+    ) = refs
+    if not head:
+        small = [operator_ref] + small
     group = range(start_ref.shape[0])
 
     def operate_right(i, vector):
@@ -112,8 +115,15 @@
         ]
         lanes_in = pltpu.make_async_copy(lanes_hbm, lanes_ref, sems.at[2])
         left_in = pltpu.make_async_copy(left_hbm, left_ref, sems.at[3])
+        small_in = [
+            pltpu.make_async_copy(hbm, ref, sems.at[6 + len(group) + k])
+            for k, (hbm, ref) in enumerate(zip([offset_hbm] + list(small_hbm), [offset_ref] + small))
+        ]
+        for copy in small_in:
+            copy.start()
         start_in.start()
-        right_in[0].start()
+        for copy in right_in:
+            copy.start()
         lanes_in.start()
 
         @pl.when(outer)
@@ -124,9 +134,18 @@
         def _():
             left_in.start()
 
-        for copy in right_in[1:]:
-            copy.start()
-        sums = before_ref[...]
+        for copy in small_in:
+            copy.wait()
+        if head:
+            mpo_ref, rows_ref, cols_ref, same_ref = small
+            sums = jnp.zeros((1, BLK), jnp.float32)
+            wide = matmul(rows_ref[...], mpo_ref[...]).astype(jnp.bfloat16)
+            wide = matmul(wide, cols_ref[...]).astype(jnp.bfloat16)
+            operator_ref[...] = wide * same_ref[...]
+            operator_out = pltpu.make_async_copy(operator_ref, operator_hbm, sems.at[6 + len(group) + 5])
+            operator_out.start()
+        else:
+            sums = small[1][...]
 
         def note(sums, i, quantity, value):
             slot = base + i
@@ -136,17 +155,17 @@
             column = jnp.broadcast_to(offset_ref[base + i:base + i + 1, :], (BLK, BLK)).T
             for s in range(PHYS):
                 shift[i, pl.ds(s, BLK, stride=PHYS), :] = column
-        start_in.wait()
-        for i in group:
-            right_in[i].wait()
-        lanes_in.wait()
-        left_in.wait()
         res_out = pltpu.make_async_copy(res_ref, res_hbm, sems.at[4])
         deep_out = pltpu.make_async_copy(deep_ref, deep_hbm, sems.at[5])
         norm, res_norm = {}, {}
 
-        for i in group:
+        start_in.wait()
+        for i in group:
+            right_in[i].wait()
             operate_right(i, start_ref[i])
+        lanes_in.wait()
+        left_in.wait()
+        for i in group:
             order_lanes(i)
         for i in group:
             first = start_ref[i].astype(jnp.float32)
@@ -158,6 +177,7 @@
             res_norm[i] = total(res * res)
             sums = note(note(note(sums, i, NORM, norm[i]), i, SHIFT, quotient), i, RES, res_norm[i])
 
+        res_out.start()
         for i in group:
             operate_right(i, res_ref[i].astype(jnp.bfloat16))
         for i in group:
@@ -170,6 +190,7 @@
             deep_ref[i] = deep
             sums = note(note(note(sums, i, BACK, back), i, DIAG, diag), i, DEEP, total(deep * deep))
 
+        deep_out.start()
         for i in group:
             operate_right(i, deep_ref[i].astype(jnp.bfloat16))
         for i in group:
@@ -178,54 +199,44 @@
             sums = note(sums, i, ON_F, total(start_ref[i].astype(jnp.float32) * image))
             sums = note(sums, i, ON_R, total(res_ref[i] * image))
             sums = note(sums, i, ON_D, total(deep * image))
-        res_out.start()
-        deep_out.start()
         sums_ref[...] = jnp.broadcast_to(sums, sums_ref.shape)
         res_out.wait()
         deep_out.wait()
-
-    @pl.when(base >= live)
-    def _():
-        sums_ref[...] = jnp.broadcast_to(before_ref[...], sums_ref.shape)
+        if head:
+            operator_out.wait()
+
+    if not head:
+
+        @pl.when(base >= live)
+        def _():
+            before_in = pltpu.make_async_copy(small_hbm[1], small[1], sems.at[0])
+            before_in.start()
+            before_in.wait()
+            sums_ref[...] = jnp.broadcast_to(small[1][...], sums_ref.shape)
 
 
 def rotate_kernel(
-    scale, slots, sectors, live_ref, all_ref, own_ref, start_hbm, *refs
+    scale, slots, sectors, live_ref, all_hbm, own_hbm, start_hbm, *refs
 ):
     groups = slots // GROUPED
     res_hbm, deep_hbm = refs[:groups], refs[groups:2 * groups]
     state_hbm, density_hbm, energy_ref = refs[2 * groups:2 * groups + 3]
-    start_ref, res_ref, deep_ref, state_ref, density_ref, spread, sems = refs[2 * groups + 3:]
+    table_ref, start_ref, res_ref, deep_ref, state_ref, density_ref, spread, sems = refs[2 * groups + 3:]
     live = live_ref[0, 0]
-
-    def coming(slot):
-        return (
-            pltpu.make_async_copy(start_hbm.at[slot], start_ref.at[slot], sems.at[0, slot]),
-            pltpu.make_async_copy(res_hbm[slot // GROUPED].at[slot % GROUPED], res_ref.at[slot], sems.at[1, slot]),
-            pltpu.make_async_copy(deep_hbm[slot // GROUPED].at[slot % GROUPED], deep_ref.at[slot], sems.at[2, slot]),
-        )
-
-    def going(slot):
-        return (
-            pltpu.make_async_copy(state_ref.at[slot], state_hbm.at[slot], sems.at[3, slot]),
-            pltpu.make_async_copy(density_ref.at[slot], density_hbm.at[slot], sems.at[4, slot]),
-        )
-
-    for slot in range(slots):
-
-        @pl.when(slot < live)
-        def _():
-            for copy in coming(slot):
-                copy.start()
-
-        @pl.when(slot >= live)
-        def _():
-            state_ref[slot] = jnp.zeros(state_ref.shape[1:], state_ref.dtype)
-            density_ref[slot] = jnp.zeros(density_ref.shape[1:], density_ref.dtype)
-            for copy in going(slot):
-                copy.start()
-
-    table = jnp.concatenate([all_ref[...], own_ref[0:8, :]], axis=0)
+    tables = [
+        pltpu.make_async_copy(all_hbm, table_ref.at[pl.ds(0, sectors)], sems.at[0, 0]),
+        pltpu.make_async_copy(own_hbm.at[pl.ds(0, 8)], table_ref.at[pl.ds(sectors, 8)], sems.at[1, 0]),
+    ]
+    coming = [pltpu.make_async_copy(start_hbm, start_ref, sems.at[2, 0])]
+    for group in range(groups):
+        rows = pl.ds(group * GROUPED, GROUPED)
+        coming.append(pltpu.make_async_copy(res_hbm[group], res_ref.at[rows], sems.at[0, 1 + group]))
+        coming.append(pltpu.make_async_copy(deep_hbm[group], deep_ref.at[rows], sems.at[1, 1 + group]))
+    for copy in tables + coming:
+        copy.start()
+    for copy in tables:
+        copy.wait()
+    table = table_ref[...]
     shape = (sectors + 8, BLK)
     row = lax.broadcasted_iota(jnp.int32, shape, 0)
     lane = lax.broadcasted_iota(jnp.int32, shape, 1)
@@ -282,31 +293,30 @@
         applied = turned + tuple(sin_part * y for y in image[3:])
     energy_ref[...] = jnp.broadcast_to(inner(current, applied), energy_ref.shape)
     mine = [scale * x[sectors:sectors + 1, :] for x in current]
+    for copy in coming:
+        copy.wait()
+    going = []
     for slot in range(slots):
-
-        @pl.when(slot < live)
-        def _():
-            for copy in coming(slot):
-                copy.wait()
-            on_first, on_res, on_deep = [x[:, slot:slot + 1] for x in mine]
-            state = on_first * start_ref[slot].astype(jnp.float32)
-            state = state + on_res * res_ref[slot] + on_deep * deep_ref[slot]
-            state = state.astype(jnp.bfloat16)
-            state_ref[slot] = state
-            spread[slot] = state.astype(jnp.float32)
-            wide = jnp.concatenate(
-                [spread[slot, pl.ds(s, BLK, stride=PHYS), :] for s in range(PHYS)], axis=1
-            ).astype(jnp.bfloat16)
-            product = lax.dot_general(
-                wide, wide, (((1,), (1,)), ((), ())), preferred_element_type=jnp.float32
-            )
-            density_ref[slot] = product * (1.0 / ROWS)
-            for copy in going(slot):
-                copy.start()
-
+        on_first, on_res, on_deep = [x[:, slot:slot + 1] for x in mine]
+        state = on_first * start_ref[slot].astype(jnp.float32)
+        state = state + on_res * res_ref[slot] + on_deep * deep_ref[slot]
+        state = jnp.where(slot < live, state, 0.0).astype(jnp.bfloat16)
+        state_ref[slot] = state
+        spread[slot] = state.astype(jnp.float32)
+        going.append(pltpu.make_async_copy(state_ref.at[slot], state_hbm.at[slot], sems.at[3, slot]))
+        going[-1].start()
     for slot in range(slots):
-        for copy in going(slot):
-            copy.wait()
+        wide = jnp.concatenate(
+            [spread[slot, pl.ds(s, BLK, stride=PHYS), :] for s in range(PHYS)], axis=1
+        ).astype(jnp.bfloat16)
+        product = lax.dot_general(
+            wide, wide, (((1,), (1,)), ((), ())), preferred_element_type=jnp.float32
+        )
+        density_ref[slot] = product * (1.0 / ROWS)
+        going.append(pltpu.make_async_copy(density_ref.at[slot], density_hbm.at[slot], sems.at[4, slot]))
+        going[-1].start()
+    for copy in going:
+        copy.wait()
 
 
 def from_behind(shard, axis, by):
@@ -330,70 +340,60 @@
     return jnp.where(second, early[:slots] * total + early[slots:], total)
 
 
-def body(start_state, left_env, right_env, mpo_tensor, decay, energy_terms, live_count):
-    slots = start_state.shape[1]
-    sectors = lax.axis_size("sector")
-    start = start_state.reshape(slots, ROWS, BLK)
-    offsets = entering(decay[0], energy_terms[0], "region")
-    arrived = [from_behind(left_env[0, at:at + GROUPED], "region", 1) for at in range(0, slots, GROUPED)]
-    region = lax.axis_index("region").reshape(1).astype(jnp.int32)
-    mpo = mpo_tensor.reshape(CHAN * PHYS, PHYS * CHAN)
-    lanes, rows, cols, same = constants()
-
-    smem = pl.BlockSpec(memory_space=pltpu.SMEM)
-    vmem = pl.BlockSpec(memory_space=pltpu.VMEM)
-    hbm = pl.BlockSpec(memory_space=pl.ANY)
+SMEM = pl.BlockSpec(memory_space=pltpu.SMEM)
+VMEM = pl.BlockSpec(memory_space=pltpu.VMEM)
+HBM = pl.BlockSpec(memory_space=pl.ANY)
+
+
+def krylov_call(base, copies, live_count, region, before, offsets, operator, start, own, left, right, lanes):
     vectors = jax.ShapeDtypeStruct((GROUPED, ROWS, BLK), jnp.float32)
-    operator = pl.pallas_call(
-        operator_kernel,
-        in_specs=[vmem] * 4,
-        out_specs=vmem,
-        out_shape=jax.ShapeDtypeStruct((256, 256), jnp.bfloat16),
-        name="operator",
-    )(mpo, rows, cols, same)
-    sums = jnp.zeros((1, BLK), jnp.float32)
-    res, deep = [], []
-    for base in range(0, slots, GROUPED):
-        copies = sectors if base + GROUPED == slots else 1
-        sums, res_one, deep_one = pl.pallas_call(
-            functools.partial(krylov_kernel, base),
-            in_specs=[smem, smem, vmem, vmem, vmem, hbm, hbm, hbm, hbm, hbm],
-            out_specs=[vmem, hbm, hbm],
-            out_shape=[jax.ShapeDtypeStruct((copies, BLK), jnp.float32), vectors, vectors],
-            scratch_shapes=[
-                pltpu.VMEM((GROUPED, ROWS, BLK), jnp.bfloat16),
-                pltpu.VMEM((GROUPED, CHAN, BLK, BLK), jnp.bfloat16),
-                pltpu.VMEM((GROUPED, CHAN, BLK, BLK), jnp.bfloat16),
-                pltpu.VMEM((4 * BLK, 4 * BLK), jnp.bfloat16),
-                pltpu.VMEM((GROUPED, ROWS, BLK), jnp.float32),
-                pltpu.VMEM((GROUPED, ROWS, BLK), jnp.float32),
-                pltpu.VMEM((GROUPED, BLK, CHAN * BLK), jnp.bfloat16),
-                pltpu.VMEM((GROUPED, 16, 256, 256), jnp.bfloat16),
-                pltpu.VMEM((GROUPED, CHAN * BLK, ROWS), jnp.bfloat16),
-                pltpu.VMEM((GROUPED, ROWS, BLK), jnp.float32),
-                pltpu.VMEM((GROUPED, ROWS, BLK), jnp.float32),
-                pltpu.SemaphoreType.DMA((6 + GROUPED,)),
-            ],
-            compiler_params=pltpu.CompilerParams(vmem_limit_bytes=VMEM_LIMIT),
-            cost_estimate=pl.CostEstimate(flops=10**10, bytes_accessed=1 << 22, transcendentals=0),
-            name="krylov",
-        )(
-            live_count, region, sums, offsets, operator,
-            start, left_env[0], arrived[base // GROUPED], right_env[0], lanes,
-        )
-        res.append(res_one)
-        deep.append(deep_one)
-    every = lax.all_to_all(sums.reshape(sectors, 1, BLK), "sector", 0, 0).reshape(sectors, BLK)
-    state, density, energy = pl.pallas_call(
+    head = base == 0
+    kernel = functools.partial(krylov_kernel, base)
+    operands = [live_count, region, offsets, start, own, left, right, lanes]
+    operands += list(operator) if head else [operator, before]
+    shapes = [jax.ShapeDtypeStruct((copies, BLK), jnp.float32), vectors, vectors]
+    shapes += [jax.ShapeDtypeStruct((256, 256), jnp.bfloat16)] if head else []
+    small = [pltpu.VMEM(x.shape, x.dtype) for x in (operator if head else [before])]
+    return pl.pallas_call(
+        kernel,
+        in_specs=[SMEM, SMEM] + [HBM] * (len(operands) - 2),
+        out_specs=[VMEM] + [HBM] * (len(shapes) - 1),
+        out_shape=shapes,
+        scratch_shapes=[
+            pltpu.VMEM((GROUPED, ROWS, BLK), jnp.bfloat16),
+            pltpu.VMEM((GROUPED, CHAN, BLK, BLK), jnp.bfloat16),
+            pltpu.VMEM((GROUPED, CHAN, BLK, BLK), jnp.bfloat16),
+            pltpu.VMEM((4 * BLK, 4 * BLK), jnp.bfloat16),
+            pltpu.VMEM((GROUPED, ROWS, BLK), jnp.float32),
+            pltpu.VMEM((GROUPED, ROWS, BLK), jnp.float32),
+            pltpu.VMEM((GROUPED, BLK, CHAN * BLK), jnp.bfloat16),
+            pltpu.VMEM((GROUPED, 16, 256, 256), jnp.bfloat16),
+            pltpu.VMEM((GROUPED, CHAN * BLK, ROWS), jnp.bfloat16),
+            pltpu.VMEM((GROUPED, ROWS, BLK), jnp.float32),
+            pltpu.VMEM((GROUPED, ROWS, BLK), jnp.float32),
+            pltpu.VMEM(offsets.shape, jnp.float32),
+            pltpu.VMEM((256, 256), jnp.bfloat16),
+            pltpu.SemaphoreType.DMA((12 + GROUPED,)),
+        ] + small,
+        compiler_params=pltpu.CompilerParams(vmem_limit_bytes=VMEM_LIMIT),
+        cost_estimate=pl.CostEstimate(flops=10**10, bytes_accessed=1 << 22, transcendentals=0),
+        name="krylov",
+    )(*operands)
+
+
+def rotate_call(sectors, live_count, every, sums, start, res, deep):
+    slots = start.shape[0]
+    return pl.pallas_call(
         functools.partial(rotate_kernel, math.sqrt(slots * sectors * ROWS * BLK), slots, sectors),
-        in_specs=[smem, vmem, vmem] + [hbm] * (1 + 2 * (slots // GROUPED)),
-        out_specs=[hbm, hbm, vmem],
+        in_specs=[SMEM] + [HBM] * (3 + 2 * (slots // GROUPED)),
+        out_specs=[HBM, HBM, VMEM],
         out_shape=[
             jax.ShapeDtypeStruct((slots, ROWS, BLK), jnp.bfloat16),
             jax.ShapeDtypeStruct((slots, BLK, BLK), jnp.float32),
             jax.ShapeDtypeStruct((1, 1), jnp.float32),
         ],
         scratch_shapes=[
+            pltpu.VMEM((sectors + 8, BLK), jnp.float32),
             pltpu.VMEM((slots, ROWS, BLK), jnp.bfloat16),
             pltpu.VMEM((slots, ROWS, BLK), jnp.float32),
             pltpu.VMEM((slots, ROWS, BLK), jnp.float32),
@@ -405,6 +405,31 @@
         compiler_params=pltpu.CompilerParams(vmem_limit_bytes=VMEM_LIMIT),
         name="rotate",
     )(live_count, every, sums, start, *res, *deep)
+
+
+def body(start_state, left_env, right_env, mpo_tensor, decay, energy_terms, live_count):
+    slots = start_state.shape[1]
+    sectors = lax.axis_size("sector")
+    start = start_state.reshape(slots, ROWS, BLK)
+    arrived = [from_behind(left_env[0, at:at + GROUPED], "region", 1) for at in range(0, slots, GROUPED)]
+    offsets = entering(decay[0], energy_terms[0], "region")
+    region = lax.axis_index("region").reshape(1).astype(jnp.int32)
+    mpo = mpo_tensor.reshape(CHAN * PHYS, PHYS * CHAN)
+    lanes, rows, cols, same = constants()
+    sums = None
+    operator = (mpo, rows, cols, same)
+    res, deep = [], []
+    for base in range(0, slots, GROUPED):
+        copies = sectors if base + GROUPED == slots else 1
+        sums, res_one, deep_one, *made = krylov_call(
+            base, copies, live_count, region, sums, offsets, operator,
+            start, left_env[0], arrived[base // GROUPED], right_env[0], lanes,
+        )
+        operator = made[0] if made else operator
+        res.append(res_one)
+        deep.append(deep_one)
+    every = lax.all_to_all(sums.reshape(sectors, 1, BLK), "sector", 0, 0).reshape(sectors, BLK)
+    state, density, energy = rotate_call(sectors, live_count, every, sums, start, res, deep)
     return (state.reshape(start_state.shape), density[None], energy.reshape(1))
 
 

time: 73.9 us -> 69.8 us (0.945)
  the two profiles are of different devices: /device:TPU:1 before, /device:TPU:6 now
where the time goes in v2:
time: 69.8 us; the launch traced here: 68.9 us
  blocking collectives  31.8 us (46%)
  Pallas kernels  17.4 us (25%)
  starting transfers between devices  8.18 us (12%)
  waiting for transfers between devices  5.88 us (8%)
  local copies, waits for them, and re-layouts  3.43 us (5%)
  between operations  1.59 us (2%)
    all_to_all x1, blocking collectives, body(): lax.all_to_all(sums.reshape(sectors, 1, BLK), 'sector', 0, 0)  31.8 us
    pallas_call x2, Pallas kernels, krylov_call(): pl.pallas_call(kernel, in_specs=[SMEM, SMEM] + [HBM] * (len(operands) - 2...  13.7 us
    ppermute x5, starting transfers between devices, from_behind(): return lax.ppermute(shard, axis, [(i, i + by) for i in range(length - by)])  8.09 us
    ppermute x5, waiting for transfers between devices, from_behind(): return lax.ppermute(shard, axis, [(i, i + by) for i in range(length - by)])  3.76 us
    pallas_call x1, Pallas kernels, rotate_call(): pl.pallas_call(functools.partial(rotate_kernel, math.sqrt(slots * sectors...  3.66 us
    ppermute x1, waiting for transfers between devices, entering(): lax.ppermute(own, axis, [(i, i ^ 1) for i in range(lax.axis_size(axis))])  2.12 us
    squeeze x1, local copies, waits for them, and re-layouts, body(): left_env[0, at:at + GROUPED]  1.71 us
  transfers between devices with their start and end apart: 6, of which 3 were waited for; matrix products, arithmetic and copies ran while one was open for 2% of the time, Pallas kernels for 18%

profile of v2, /device:TPU:6, one launch (start us, length us, event | category | flops | bytes accessed | tf_op | source)
XLA Modules:
  0.0 68.9 jit_solution(3716470349467808880)
XLA Ops:
  0.6 0.0 copy-start.1
  0.6 0.0 copy-start.2
  0.7 0.0 copy-start
  0.7 1.7 %slice_bitcast_fusion = (bf16[2,16,128,128]{3,2,1,0:T(8,128)(2,1)S(1)}, bf16[2,16,128,128]{3,2,1,0:T(8,128)(2,1)S(1)}) fusion(bf16[1,4,16,128,128]{4,3,2,1,0:T(8,128)(2,1)} %param.12), kind=kLoop, calls=%fused_computation | loop fusion | bytes 4194304 | tf_op jit(solution)/shard_map/squeeze | solution.py:414
  2.4 1.9 %collective-permute-start.5 = (bf16[2,16,128,128]{3,2,1,0:T(8,128)(2,1)S(1)}, bf16[2,16,128,128]{3,2,1,0:T(8,128)(2,1)S(1)}, u32[]{:S(2)}, u32[]{:S(2)}) collective-permute-start(bf16[2,16,128,128]{3,2,1,0:T(8,128)(2,1)S(1)} %get-tuple-element.23), channel_id=1, source_target_pairs={{0,32},{32,64},{64,96},{96,128},{128,160},{160,192},{192,224},{1,3... | collective-permute-start | bytes 3145736 | tf_op jit(solution)/shard_map/ppermute | solution.py:324
  4.3 0.0 copy-done.1
  4.3 0.0 copy-done.2
  4.3 0.1 collective-permute-start
  4.5 2.1 %collective-permute-done = f32[8,128]{1,0:T(8,128)S(1)} collective-permute-done((f32[8,128]{1,0:T(8,128)S(1)}, f32[8,128]{1,0:T(8,128)S(1)}, u32[]{:S(2)}, u32[]{:S(2)}) %collective-permute-start) | collective-permute-done | bytes 4128 | tf_op jit(solution)/shard_map/ppermute | solution.py:330
  6.6 1.3 %collective-permute-start.3 = (f32[8,128]{1,0:T(8,128)S(1)}, f32[8,128]{1,0:T(8,128)S(1)}, u32[]{:S(2)}, u32[]{:S(2)}) collective-permute-start(f32[8,128]{1,0:T(8,128)S(1)} %pad_maximum_fusion.1), channel_id=1, source_target_pairs={{0,192},{32,224},{1,193},{33,225},{2,194},{34,226},{3,195},{35,227... | collective-permute-start | bytes 12296 | tf_op jit(solution)/shard_map/ppermute | solution.py:324
  7.9 1.3 %collective-permute-start.2 = (f32[8,128]{1,0:T(8,128)S(1)}, f32[8,128]{1,0:T(8,128)S(1)}, u32[]{:S(2)}, u32[]{:S(2)}) collective-permute-start(f32[8,128]{1,0:T(8,128)S(1)} %pad_maximum_fusion.1), channel_id=1, source_target_pairs={{0,128},{32,160},{64,192},{96,224},{1,129},{33,161},{65,193},{97,2... | collective-permute-start | bytes 12296 | tf_op jit(solution)/shard_map/ppermute | solution.py:324
  9.2 1.3 %collective-permute-start.1 = (f32[8,128]{1,0:T(8,128)S(1)}, f32[8,128]{1,0:T(8,128)S(1)}, u32[]{:S(2)}, u32[]{:S(2)}) collective-permute-start(f32[8,128]{1,0:T(8,128)S(1)} %pad_maximum_fusion.1), channel_id=1, source_target_pairs={{0,64},{32,96},{64,128},{96,160},{128,192},{160,224},{1,65},{33,97... | collective-permute-start | bytes 12296 | tf_op jit(solution)/shard_map/ppermute | solution.py:324
  10.5 2.3 %collective-permute-start.4 = (bf16[2,16,128,128]{3,2,1,0:T(8,128)(2,1)S(1)}, bf16[2,16,128,128]{3,2,1,0:T(8,128)(2,1)}, u32[]{:S(2)}, u32[]{:S(2)}) collective-permute-start(bf16[2,16,128,128]{3,2,1,0:T(8,128)(2,1)S(1)} %get-tuple-element.24), channel_id=1, source_target_pairs={{0,32},{32,64},{64,96},{96,128},{128,160},{160,192},{192,224},{1,3... | collective-permute-start | bytes 3145736 | tf_op jit(solution)/shard_map/ppermute | solution.py:324
  13.5 0.0 copy-done
  13.5 0.7 %reshape.29.refs_0_ = bf16[64,64]{1,0:T(8,128)(2,1)} reshape(bf16[16,4,4,16]{3,2,1,0:T(4,128)(2,1)S(1)} %copy-done) | data formatting | bytes 16384 | tf_op jit(solution)/shard_map/reshape | solution.py:417
  14.2 0.0 collective-permute-done.3
  14.2 0.8 %collective-permute-done.2 = f32[8,128]{1,0:T(8,128)S(1)} collective-permute-done((f32[8,128]{1,0:T(8,128)S(1)}, f32[8,128]{1,0:T(8,128)S(1)}, u32[]{:S(2)}, u32[]{:S(2)}) %collective-permute-start.2) | collective-permute-done | bytes 4128 | tf_op jit(solution)/shard_map/ppermute | solution.py:324
  14.9 0.0 collective-permute-done.1
  14.9 0.6 add_select_fusion.offset_hbm
  15.5 3.0 %collective-permute-done.5.left_hbm = bf16[2,16,128,128]{3,2,1,0:T(8,128)(2,1)S(1)} collective-permute-done((bf16[2,16,128,128]{3,2,1,0:T(8,128)(2,1)S(1)}, bf16[2,16,128,128]{3,2,1,0:T(8,128)(2,1)S(1)}, u32[]{:S(2)}, u32[]{:S(2)}) %collective-permute-start.5) | collective-permute-done | bytes 1048608 | tf_op jit(solution)/shard_map/ppermute | solution.py:324
  18.5 0.0 copy-start.3
  18.5 1.0 %copy-done.3 = bf16[2,16,128,128]{3,2,1,0:T(8,128)(2,1)} copy-done((bf16[2,16,128,128]{3,2,1,0:T(8,128)(2,1)}, bf16[2,16,128,128]{3,2,1,0:T(8,128)(2,1)S(1)}, u32[]{:S(2)}) %copy-start.3) | copy-done | bytes 1048600
  19.5 12.1 %krylov.2 = (f32[1,128]{1,0:T(1,128)}, f32[2,512,128]{2,1,0:T(8,128)}, f32[2,512,128]{2,1,0:T(8,128)}, bf16[256,256]{1,0:T(8,128)(2,1)}) custom-call(s32[1,1]{1,0:T(1,128)S(6)} %copy.15.live_ref, s32[1]{0:T(128)} %bitcast.region_ref, f32[4,128]{1,0:T(4,128)} %add_select_fusion.offset_hbm, bf16[4,512,128]{2,1,0:T(8,128)(2,1)} %bitcast.19, ...), custom_call_target="tpu_custom_call" | custom-call | flops 10000000000 | bytes 4194304 | tf_op jit(solution)/shard_map/krylov/pallas_call | solution.py:357
  31.7 0.0 collective-permute-done.4.left_hbm
  31.7 1.6 %krylov.3 = (f32[32,128]{1,0:T(8,128)}, f32[2,512,128]{2,1,0:T(8,128)}, f32[2,512,128]{2,1,0:T(8,128)}) custom-call(s32[1,1]{1,0:T(1,128)S(6)} %copy.15.live_ref, s32[1]{0:T(128)} %bitcast.region_ref, f32[4,128]{1,0:T(4,128)} %add_select_fusion.offset_hbm, bf16[4,512,128]{2,1,0:T(8,128)(2,1)} %bitcast.20, bf16[4,16,128,128]{3,2,1,0:T(8,128)(2,1)} %bitcast.18, ...), custom_call_target="tpu_custom_call" | custom-call | flops 10000000000 | bytes 4194304 | tf_op jit(solution)/shard_map/krylov/pallas_call | solution.py:357
  33.3 31.8 %all_to_all.5 = f32[32,1,128]{2,1,0:T(1,128)} all-to-all(f32[32,1,128]{2,1,0:T(1,128)} %bitcast.22), channel_id=1, replica_groups=mesh['region'=8,'sector'=32] {'sector'}, dimensions={0} | all-to-all | bytes 32768 | tf_op jit(solution)/shard_map/all_to_all | solution.py:431
  65.1 3.7 %rotate.1 = (bf16[4,512,128]{2,1,0:T(8,128)(2,1)}, f32[4,128,128]{2,1,0:T(8,128)}, f32[1,1]{1,0:T(1,128)}) custom-call(s32[1,1]{1,0:T(1,128)S(6)} %copy.15.live_ref, f32[32,128]{1,0:T(8,128)} %bitcast.23, f32[32,128]{1,0:T(8,128)} %get-tuple-element.15.own_hbm, bf16[4,512,128]{2,1,0:T(8,128)(2,1)} %bitcast.21, f32[2,512,128]{2,1,0:T(8,128)} %get-tuple-element.16.refs_0_, ...), custom_call_target="tpu_custom_call" | custom-call | tf_op jit(solution)/shard_map/rotate/pallas_call | solution.py:386
  (4 shorter events, 0.0 us)
Async XLA Ops:
  0.6 3.7 %copy-start.1 = (f32[1,4,128]{2,1,0:T(4,128)S(1)}, f32[1,4,128]{2,1,0:T(4,128)}, u32[]{:S(2)}) copy-start(f32[1,4,128]{2,1,0:T(4,128)} %param.16) | copy-start | bytes 6148
  0.6 3.7 %copy-start.2 = (f32[1,4,128]{2,1,0:T(4,128)S(1)}, f32[1,4,128]{2,1,0:T(4,128)}, u32[]{:S(2)}) copy-start(f32[1,4,128]{2,1,0:T(4,128)} %param.15) | copy-start | bytes 6148
  0.7 12.8 %copy-start = (bf16[16,4,4,16]{3,2,1,0:T(4,128)(2,1)S(1)}, bf16[16,4,4,16]{3,2,1,0:T(4,128)(2,1)}, u32[]{:S(2)}) copy-start(bf16[16,4,4,16]{3,2,1,0:T(4,128)(2,1)} %param.14) | copy-start | bytes 24580
  2.4 16.2 %collective-permute-start.5 = (bf16[2,16,128,128]{3,2,1,0:T(8,128)(2,1)S(1)}, bf16[2,16,128,128]{3,2,1,0:T(8,128)(2,1)S(1)}, u32[]{:S(2)}, u32[]{:S(2)}) collective-permute-start(bf16[2,16,128,128]{3,2,1,0:T(8,128)(2,1)S(1)} %get-tuple-element.23), channel_id=1, source_target_pairs={{0,32},{32,64},{64,96},{96,128},{128,160},{160,192},{192,224},{1,3... | collective-permute-start | bytes 3145736 | tf_op jit(solution)/shard_map/ppermute | solution.py:324
  4.3 2.2 %collective-permute-start = (f32[8,128]{1,0:T(8,128)S(1)}, f32[8,128]{1,0:T(8,128)S(1)}, u32[]{:S(2)}, u32[]{:S(2)}) collective-permute-start(f32[8,128]{1,0:T(8,128)S(1)} %pad_maximum_fusion), channel_id=1, source_target_pairs={{0,32},{32,0},{64,96},{96,64},{128,160},{160,128},{192,224},{224,1... | collective-permute-start | bytes 12296 | tf_op jit(solution)/shard_map/ppermute | solution.py:330
  6.6 7.6 %collective-permute-start.3 = (f32[8,128]{1,0:T(8,128)S(1)}, f32[8,128]{1,0:T(8,128)S(1)}, u32[]{:S(2)}, u32[]{:S(2)}) collective-permute-start(f32[8,128]{1,0:T(8,128)S(1)} %pad_maximum_fusion.1), channel_id=1, source_target_pairs={{0,192},{32,224},{1,193},{33,225},{2,194},{34,226},{3,195},{35,227... | collective-permute-start | bytes 12296 | tf_op jit(solution)/shard_map/ppermute | solution.py:324
  7.9 7.0 %collective-permute-start.2 = (f32[8,128]{1,0:T(8,128)S(1)}, f32[8,128]{1,0:T(8,128)S(1)}, u32[]{:S(2)}, u32[]{:S(2)}) collective-permute-start(f32[8,128]{1,0:T(8,128)S(1)} %pad_maximum_fusion.1), channel_id=1, source_target_pairs={{0,128},{32,160},{64,192},{96,224},{1,129},{33,161},{65,193},{97,2... | collective-permute-start | bytes 12296 | tf_op jit(solution)/shard_map/ppermute | solution.py:324
  9.2 5.7 %collective-permute-start.1 = (f32[8,128]{1,0:T(8,128)S(1)}, f32[8,128]{1,0:T(8,128)S(1)}, u32[]{:S(2)}, u32[]{:S(2)}) collective-permute-start(f32[8,128]{1,0:T(8,128)S(1)} %pad_maximum_fusion.1), channel_id=1, source_target_pairs={{0,64},{32,96},{64,128},{96,160},{128,192},{160,224},{1,65},{33,97... | collective-permute-start | bytes 12296 | tf_op jit(solution)/shard_map/ppermute | solution.py:324
  10.5 21.2 %collective-permute-start.4 = (bf16[2,16,128,128]{3,2,1,0:T(8,128)(2,1)S(1)}, bf16[2,16,128,128]{3,2,1,0:T(8,128)(2,1)}, u32[]{:S(2)}, u32[]{:S(2)}) collective-permute-start(bf16[2,16,128,128]{3,2,1,0:T(8,128)(2,1)S(1)} %get-tuple-element.24), channel_id=1, source_target_pairs={{0,32},{32,64},{64,96},{96,128},{128,160},{160,192},{192,224},{1,3... | collective-permute-start | bytes 3145736 | tf_op jit(solution)/shard_map/ppermute | solution.py:324
  18.5 1.0 %copy-start.3 = (bf16[2,16,128,128]{3,2,1,0:T(8,128)(2,1)}, bf16[2,16,128,128]{3,2,1,0:T(8,128)(2,1)S(1)}, u32[]{:S(2)}) copy-start(bf16[2,16,128,128]{3,2,1,0:T(8,128)(2,1)S(1)} %collective-permute-done.5.left_hbm) | copy-start | bytes 3145732

commit v3 on v2

--- a/solution.py
+++ b/solution.py
@@ -16,7 +16,7 @@
 CHAN = 16
 ROWS = BLK * PHYS
 GROUP = 4
-VMEM_LIMIT = 56 << 20
+VMEM_LIMIT = 61 << 20
 GROUPED = 2
 STRIDE = 8
 

time: 69.8 us -> 69 us (0.989)
  local copies, waits for them, and re-layouts: 3.43 us -> 2.54 us
    unnamed x8 -> x6, local copies, waits for them, and re-layouts: 1 us -> 0.01 us
where the time goes in v3:
time: 69 us; the launch traced here: 68.1 us
  blocking collectives  31.8 us (46%)
  Pallas kernels  17.4 us (25%)
  starting transfers between devices  8.18 us (12%)
  waiting for transfers between devices  5.99 us (9%)
  local copies, waits for them, and re-layouts  2.54 us (4%)
  between operations  1.59 us (2%)
    all_to_all x1, blocking collectives, body(): lax.all_to_all(sums.reshape(sectors, 1, BLK), 'sector', 0, 0)  31.8 us
    pallas_call x2, Pallas kernels, krylov_call(): pl.pallas_call(kernel, in_specs=[SMEM, SMEM] + [HBM] * (len(operands) - 2...  13.7 us
    ppermute x5, starting transfers between devices, from_behind(): return lax.ppermute(shard, axis, [(i, i + by) for i in range(length - by)])  8.09 us
    ppermute x5, waiting for transfers between devices, from_behind(): return lax.ppermute(shard, axis, [(i, i + by) for i in range(length - by)])  3.86 us
    pallas_call x1, Pallas kernels, rotate_call(): pl.pallas_call(functools.partial(rotate_kernel, math.sqrt(slots * sectors...  3.66 us
    ppermute x1, waiting for transfers between devices, entering(): lax.ppermute(own, axis, [(i, i ^ 1) for i in range(lax.axis_size(axis))])  2.12 us
    squeeze x1, local copies, waits for them, and re-layouts, body(): left_env[0, at:at + GROUPED]  1.81 us
  transfers between devices with their start and end apart: 6, of which 3 were waited for; matrix products, arithmetic and copies ran while one was open for 2% of the time, Pallas kernels for 18%

profile of v3, /device:TPU:6, one launch (start us, length us, event | category | flops | bytes accessed | tf_op | source)
XLA Modules:
  0.0 68.1 jit_solution(11952385167925107116)
XLA Ops:
  0.6 0.0 copy-start.1
  0.6 0.0 copy-start.2
  0.7 0.0 copy-start
  0.7 1.8 %slice_bitcast_fusion = (bf16[2,16,128,128]{3,2,1,0:T(8,128)(2,1)S(1)}, bf16[2,16,128,128]{3,2,1,0:T(8,128)(2,1)S(1)}) fusion(bf16[1,4,16,128,128]{4,3,2,1,0:T(8,128)(2,1)} %param.12), kind=kLoop, calls=%fused_computation | loop fusion | bytes 4194304 | tf_op jit(solution)/shard_map/squeeze | solution.py:414
  2.5 1.9 %collective-permute-start.5 = (bf16[2,16,128,128]{3,2,1,0:T(8,128)(2,1)S(1)}, bf16[2,16,128,128]{3,2,1,0:T(8,128)(2,1)}, u32[]{:S(2)}, u32[]{:S(2)}) collective-permute-start(bf16[2,16,128,128]{3,2,1,0:T(8,128)(2,1)S(1)} %get-tuple-element.23), channel_id=1, source_target_pairs={{0,32},{32,64},{64,96},{96,128},{128,160},{160,192},{192,224},{1,3... | collective-permute-start | bytes 3145736 | tf_op jit(solution)/shard_map/ppermute | solution.py:324
  4.4 0.0 copy-done.1
  4.4 0.0 copy-done.2
  4.4 0.1 collective-permute-start
  4.6 2.1 %collective-permute-done = f32[8,128]{1,0:T(8,128)S(1)} collective-permute-done((f32[8,128]{1,0:T(8,128)S(1)}, f32[8,128]{1,0:T(8,128)S(1)}, u32[]{:S(2)}, u32[]{:S(2)}) %collective-permute-start) | collective-permute-done | bytes 4128 | tf_op jit(solution)/shard_map/ppermute | solution.py:330
  6.7 1.3 %collective-permute-start.3 = (f32[8,128]{1,0:T(8,128)S(1)}, f32[8,128]{1,0:T(8,128)S(1)}, u32[]{:S(2)}, u32[]{:S(2)}) collective-permute-start(f32[8,128]{1,0:T(8,128)S(1)} %pad_maximum_fusion.1), channel_id=1, source_target_pairs={{0,192},{32,224},{1,193},{33,225},{2,194},{34,226},{3,195},{35,227... | collective-permute-start | bytes 12296 | tf_op jit(solution)/shard_map/ppermute | solution.py:324
  8.0 1.3 %collective-permute-start.2 = (f32[8,128]{1,0:T(8,128)S(1)}, f32[8,128]{1,0:T(8,128)S(1)}, u32[]{:S(2)}, u32[]{:S(2)}) collective-permute-start(f32[8,128]{1,0:T(8,128)S(1)} %pad_maximum_fusion.1), channel_id=1, source_target_pairs={{0,128},{32,160},{64,192},{96,224},{1,129},{33,161},{65,193},{97,2... | collective-permute-start | bytes 12296 | tf_op jit(solution)/shard_map/ppermute | solution.py:324
  9.3 1.3 %collective-permute-start.1 = (f32[8,128]{1,0:T(8,128)S(1)}, f32[8,128]{1,0:T(8,128)S(1)}, u32[]{:S(2)}, u32[]{:S(2)}) collective-permute-start(f32[8,128]{1,0:T(8,128)S(1)} %pad_maximum_fusion.1), channel_id=1, source_target_pairs={{0,64},{32,96},{64,128},{96,160},{128,192},{160,224},{1,65},{33,97... | collective-permute-start | bytes 12296 | tf_op jit(solution)/shard_map/ppermute | solution.py:324
  10.6 2.3 %collective-permute-start.4 = (bf16[2,16,128,128]{3,2,1,0:T(8,128)(2,1)S(1)}, bf16[2,16,128,128]{3,2,1,0:T(8,128)(2,1)}, u32[]{:S(2)}, u32[]{:S(2)}) collective-permute-start(bf16[2,16,128,128]{3,2,1,0:T(8,128)(2,1)S(1)} %get-tuple-element.24), channel_id=1, source_target_pairs={{0,32},{32,64},{64,96},{96,128},{128,160},{160,192},{192,224},{1,3... | collective-permute-start | bytes 3145736 | tf_op jit(solution)/shard_map/ppermute | solution.py:324
  13.6 0.0 copy-done
  13.6 0.7 %reshape.29.refs_0_ = bf16[64,64]{1,0:T(8,128)(2,1)} reshape(bf16[16,4,4,16]{3,2,1,0:T(4,128)(2,1)S(1)} %copy-done) | data formatting | bytes 16384 | tf_op jit(solution)/shard_map/reshape | solution.py:417
  14.3 0.0 collective-permute-done.3
  14.3 0.8 %collective-permute-done.2 = f32[8,128]{1,0:T(8,128)S(1)} collective-permute-done((f32[8,128]{1,0:T(8,128)S(1)}, f32[8,128]{1,0:T(8,128)S(1)}, u32[]{:S(2)}, u32[]{:S(2)}) %collective-permute-start.2) | collective-permute-done | bytes 4128 | tf_op jit(solution)/shard_map/ppermute | solution.py:324
  15.0 0.0 collective-permute-done.1
  15.0 0.6 add_select_fusion.offset_hbm
  15.6 3.1 %collective-permute-done.5.left_hbm = bf16[2,16,128,128]{3,2,1,0:T(8,128)(2,1)} collective-permute-done((bf16[2,16,128,128]{3,2,1,0:T(8,128)(2,1)S(1)}, bf16[2,16,128,128]{3,2,1,0:T(8,128)(2,1)}, u32[]{:S(2)}, u32[]{:S(2)}) %collective-permute-start.5) | collective-permute-done | bytes 1048608 | tf_op jit(solution)/shard_map/ppermute | solution.py:324
  18.7 12.1 %krylov.2 = (f32[1,128]{1,0:T(1,128)}, f32[2,512,128]{2,1,0:T(8,128)}, f32[2,512,128]{2,1,0:T(8,128)}, bf16[256,256]{1,0:T(8,128)(2,1)}) custom-call(s32[1,1]{1,0:T(1,128)S(6)} %copy.15.live_ref, s32[1]{0:T(128)} %bitcast.region_ref, f32[4,128]{1,0:T(4,128)} %add_select_fusion.offset_hbm, bf16[4,512,128]{2,1,0:T(8,128)(2,1)} %bitcast.19, ...), custom_call_target="tpu_custom_call" | custom-call | flops 10000000000 | bytes 4194304 | tf_op jit(solution)/shard_map/krylov/pallas_call | solution.py:357
  30.9 0.0 collective-permute-done.4.left_hbm
  30.9 1.6 %krylov.3 = (f32[32,128]{1,0:T(8,128)}, f32[2,512,128]{2,1,0:T(8,128)}, f32[2,512,128]{2,1,0:T(8,128)}) custom-call(s32[1,1]{1,0:T(1,128)S(6)} %copy.15.live_ref, s32[1]{0:T(128)} %bitcast.region_ref, f32[4,128]{1,0:T(4,128)} %add_select_fusion.offset_hbm, bf16[4,512,128]{2,1,0:T(8,128)(2,1)} %bitcast.20, bf16[4,16,128,128]{3,2,1,0:T(8,128)(2,1)} %bitcast.18, ...), custom_call_target="tpu_custom_call" | custom-call | flops 10000000000 | bytes 4194304 | tf_op jit(solution)/shard_map/krylov/pallas_call | solution.py:357
  32.5 31.8 %all_to_all.5 = f32[32,1,128]{2,1,0:T(1,128)} all-to-all(f32[32,1,128]{2,1,0:T(1,128)} %bitcast.22), channel_id=1, replica_groups=mesh['region'=8,'sector'=32] {'sector'}, dimensions={0} | all-to-all | bytes 32768 | tf_op jit(solution)/shard_map/all_to_all | solution.py:431
  64.3 3.7 %rotate.1 = (bf16[4,512,128]{2,1,0:T(8,128)(2,1)}, f32[4,128,128]{2,1,0:T(8,128)}, f32[1,1]{1,0:T(1,128)}) custom-call(s32[1,1]{1,0:T(1,128)S(6)} %copy.15.live_ref, f32[32,128]{1,0:T(8,128)} %bitcast.23, f32[32,128]{1,0:T(8,128)} %get-tuple-element.15.own_hbm, bf16[4,512,128]{2,1,0:T(8,128)(2,1)} %bitcast.21, f32[2,512,128]{2,1,0:T(8,128)} %get-tuple-element.16.refs_0_, ...), custom_call_target="tpu_custom_call" | custom-call | tf_op jit(solution)/shard_map/rotate/pallas_call | solution.py:386
  (4 shorter events, 0.0 us)
Async XLA Ops:
  0.6 3.8 %copy-start.1 = (f32[1,4,128]{2,1,0:T(4,128)S(1)}, f32[1,4,128]{2,1,0:T(4,128)}, u32[]{:S(2)}) copy-start(f32[1,4,128]{2,1,0:T(4,128)} %param.16) | copy-start | bytes 6148
  0.6 3.8 %copy-start.2 = (f32[1,4,128]{2,1,0:T(4,128)S(1)}, f32[1,4,128]{2,1,0:T(4,128)}, u32[]{:S(2)}) copy-start(f32[1,4,128]{2,1,0:T(4,128)} %param.15) | copy-start | bytes 6148
  0.7 12.9 %copy-start = (bf16[16,4,4,16]{3,2,1,0:T(4,128)(2,1)S(1)}, bf16[16,4,4,16]{3,2,1,0:T(4,128)(2,1)}, u32[]{:S(2)}) copy-start(bf16[16,4,4,16]{3,2,1,0:T(4,128)(2,1)} %param.14) | copy-start | bytes 24580
  2.5 16.3 %collective-permute-start.5 = (bf16[2,16,128,128]{3,2,1,0:T(8,128)(2,1)S(1)}, bf16[2,16,128,128]{3,2,1,0:T(8,128)(2,1)}, u32[]{:S(2)}, u32[]{:S(2)}) collective-permute-start(bf16[2,16,128,128]{3,2,1,0:T(8,128)(2,1)S(1)} %get-tuple-element.23), channel_id=1, source_target_pairs={{0,32},{32,64},{64,96},{96,128},{128,160},{160,192},{192,224},{1,3... | collective-permute-start | bytes 3145736 | tf_op jit(solution)/shard_map/ppermute | solution.py:324
  4.4 2.2 %collective-permute-start = (f32[8,128]{1,0:T(8,128)S(1)}, f32[8,128]{1,0:T(8,128)S(1)}, u32[]{:S(2)}, u32[]{:S(2)}) collective-permute-start(f32[8,128]{1,0:T(8,128)S(1)} %pad_maximum_fusion), channel_id=1, source_target_pairs={{0,32},{32,0},{64,96},{96,64},{128,160},{160,128},{192,224},{224,1... | collective-permute-start | bytes 12296 | tf_op jit(solution)/shard_map/ppermute | solution.py:330
  6.7 7.6 %collective-permute-start.3 = (f32[8,128]{1,0:T(8,128)S(1)}, f32[8,128]{1,0:T(8,128)S(1)}, u32[]{:S(2)}, u32[]{:S(2)}) collective-permute-start(f32[8,128]{1,0:T(8,128)S(1)} %pad_maximum_fusion.1), channel_id=1, source_target_pairs={{0,192},{32,224},{1,193},{33,225},{2,194},{34,226},{3,195},{35,227... | collective-permute-start | bytes 12296 | tf_op jit(solution)/shard_map/ppermute | solution.py:324
  8.0 7.0 %collective-permute-start.2 = (f32[8,128]{1,0:T(8,128)S(1)}, f32[8,128]{1,0:T(8,128)S(1)}, u32[]{:S(2)}, u32[]{:S(2)}) collective-permute-start(f32[8,128]{1,0:T(8,128)S(1)} %pad_maximum_fusion.1), channel_id=1, source_target_pairs={{0,128},{32,160},{64,192},{96,224},{1,129},{33,161},{65,193},{97,2... | collective-permute-start | bytes 12296 | tf_op jit(solution)/shard_map/ppermute | solution.py:324
  9.3 5.7 %collective-permute-start.1 = (f32[8,128]{1,0:T(8,128)S(1)}, f32[8,128]{1,0:T(8,128)S(1)}, u32[]{:S(2)}, u32[]{:S(2)}) collective-permute-start(f32[8,128]{1,0:T(8,128)S(1)} %pad_maximum_fusion.1), channel_id=1, source_target_pairs={{0,64},{32,96},{64,128},{96,160},{128,192},{160,224},{1,65},{33,97... | collective-permute-start | bytes 12296 | tf_op jit(solution)/shard_map/ppermute | solution.py:324
  10.6 20.3 %collective-permute-start.4 = (bf16[2,16,128,128]{3,2,1,0:T(8,128)(2,1)S(1)}, bf16[2,16,128,128]{3,2,1,0:T(8,128)(2,1)}, u32[]{:S(2)}, u32[]{:S(2)}) collective-permute-start(bf16[2,16,128,128]{3,2,1,0:T(8,128)(2,1)S(1)} %get-tuple-element.24), channel_id=1, source_target_pairs={{0,32},{32,64},{64,96},{96,128},{128,160},{160,192},{192,224},{1,3... | collective-permute-start | bytes 3145736 | tf_op jit(solution)/shard_map/ppermute | solution.py:324

commit v4 on v3

--- a/solution.py
+++ b/solution.py
@@ -16,7 +16,7 @@
 CHAN = 16
 ROWS = BLK * PHYS
 GROUP = 4
-VMEM_LIMIT = 61 << 20
+VMEM_LIMIT = 50 << 20
 GROUPED = 2
 STRIDE = 8
 

time: 69 us -> 69.9 us (1.013)
  Pallas kernels: 17.4 us -> 15.9 us
  blocking collectives: 31.8 us -> 33.2 us
  waiting for transfers between devices: 5.99 us -> 7.28 us
  local copies, waits for them, and re-layouts: 2.54 us -> 3.36 us
    squeeze x1, local copies, waits for them, and re-layouts: 1.81 us -> 3.22 us  [body(): left_env[0, at:at + GROUPED]]
    all_to_all x1, blocking collectives: 31.8 us -> 33.2 us  [body(): lax.all_to_all(sums.reshape(sectors, 1, BLK), 'sector', 0, 0)]
    ppermute x5, waiting for transfers between devices: 3.86 us -> 5.16 us  [from_behind(): return lax.ppermute(shard, axis, [(i, i + by) for i in range(length - by)])]
    pallas_call x2, Pallas kernels: 13.7 us -> 12.9 us  [krylov_call(): pl.pallas_call(kernel, in_specs=[SMEM, SMEM] + [HBM] * (len(operands) - 2...]
  transfers between devices with their start and end apart: 6 -> 6, of which waited for: 3 -> 3; matrix products, arithmetic and copies ran while one was open for 2% -> 0% of each run, Pallas kernels for 18% -> 18%
where the time goes in v4:
time: 69.9 us; the launch traced here: 69.6 us
  blocking collectives  33.2 us (47%)
  Pallas kernels  15.9 us (23%)
  starting transfers between devices  8.17 us (12%)
  waiting for transfers between devices  7.28 us (10%)
  local copies, waits for them, and re-layouts  3.36 us (5%)
  between operations  1.68 us (2%)
    all_to_all x1, blocking collectives, body(): lax.all_to_all(sums.reshape(sectors, 1, BLK), 'sector', 0, 0)  33.2 us
    pallas_call x2, Pallas kernels, krylov_call(): pl.pallas_call(kernel, in_specs=[SMEM, SMEM] + [HBM] * (len(operands) - 2...  12.9 us
    ppermute x5, starting transfers between devices, from_behind(): return lax.ppermute(shard, axis, [(i, i + by) for i in range(length - by)])  8.07 us
    ppermute x5, waiting for transfers between devices, from_behind(): return lax.ppermute(shard, axis, [(i, i + by) for i in range(length - by)])  5.16 us
    squeeze x1, local copies, waits for them, and re-layouts, body(): left_env[0, at:at + GROUPED]  3.22 us
    pallas_call x1, Pallas kernels, rotate_call(): pl.pallas_call(functools.partial(rotate_kernel, math.sqrt(slots * sectors...  3.03 us
    ppermute x1, waiting for transfers between devices, entering(): lax.ppermute(own, axis, [(i, i ^ 1) for i in range(lax.axis_size(axis))])  2.12 us
  transfers between devices with their start and end apart: 6, of which 3 were waited for; matrix products, arithmetic and copies ran while one was open for 0% of the time, Pallas kernels for 18%

profile of v4, /device:TPU:6, one launch (start us, length us, event | category | flops | bytes accessed | tf_op | source)
XLA Modules:
  0.0 69.6 jit_solution(10527461732809347970)
XLA Ops:
  0.6 0.0 copy-start.1
  0.6 0.0 copy-start.2
  0.7 0.0 copy-start.3
  0.7 0.0 copy-start.4
  0.7 0.0 copy-start.6
  0.7 0.0 copy-start.7
  0.7 0.0 copy-start.5
  0.7 0.0 copy-start
  0.7 3.2 %slice_bitcast_fusion = (bf16[2,16,128,128]{3,2,1,0:T(8,128)(2,1)}, bf16[2,16,128,128]{3,2,1,0:T(8,128)(2,1)}) fusion(bf16[1,4,16,128,128]{4,3,2,1,0:T(8,128)(2,1)} %param.12), kind=kLoop, calls=%fused_computation | loop fusion | bytes 4194304 | tf_op jit(solution)/shard_map/squeeze | solution.py:414
  3.9 1.9 %collective-permute-start.5 = (bf16[2,16,128,128]{3,2,1,0:T(8,128)(2,1)}, bf16[2,16,128,128]{3,2,1,0:T(8,128)(2,1)S(1)}, u32[]{:S(2)}, u32[]{:S(2)}) collective-permute-start(bf16[2,16,128,128]{3,2,1,0:T(8,128)(2,1)} %get-tuple-element.23), channel_id=1, source_target_pairs={{0,32},{32,64},{64,96},{96,128},{128,160},{160,192},{192,224},{1,3... | collective-permute-start | bytes 3145736 | tf_op jit(solution)/shard_map/ppermute | solution.py:324
  5.9 0.0 copy-done.6
  5.9 0.0 copy-done.7
  5.9 0.1 collective-permute-start
  6.0 2.1 %collective-permute-done = f32[8,128]{1,0:T(8,128)S(1)} collective-permute-done((f32[8,128]{1,0:T(8,128)S(1)}, f32[8,128]{1,0:T(8,128)S(1)}, u32[]{:S(2)}, u32[]{:S(2)}) %collective-permute-start) | collective-permute-done | bytes 4128 | tf_op jit(solution)/shard_map/ppermute | solution.py:330
  8.2 1.3 %collective-permute-start.3 = (f32[8,128]{1,0:T(8,128)S(1)}, f32[8,128]{1,0:T(8,128)S(1)}, u32[]{:S(2)}, u32[]{:S(2)}) collective-permute-start(f32[8,128]{1,0:T(8,128)S(1)} %pad_maximum_fusion.1), channel_id=1, source_target_pairs={{0,192},{32,224},{1,193},{33,225},{2,194},{34,226},{3,195},{35,227... | collective-permute-start | bytes 12296 | tf_op jit(solution)/shard_map/ppermute | solution.py:324
  9.5 1.3 %collective-permute-start.2 = (f32[8,128]{1,0:T(8,128)S(1)}, f32[8,128]{1,0:T(8,128)S(1)}, u32[]{:S(2)}, u32[]{:S(2)}) collective-permute-start(f32[8,128]{1,0:T(8,128)S(1)} %pad_maximum_fusion.1), channel_id=1, source_target_pairs={{0,128},{32,160},{64,192},{96,224},{1,129},{33,161},{65,193},{97,2... | collective-permute-start | bytes 12296 | tf_op jit(solution)/shard_map/ppermute | solution.py:324
  10.8 1.3 %collective-permute-start.1 = (f32[8,128]{1,0:T(8,128)S(1)}, f32[8,128]{1,0:T(8,128)S(1)}, u32[]{:S(2)}, u32[]{:S(2)}) collective-permute-start(f32[8,128]{1,0:T(8,128)S(1)} %pad_maximum_fusion.1), channel_id=1, source_target_pairs={{0,64},{32,96},{64,128},{96,160},{128,192},{160,224},{1,65},{33,97... | collective-permute-start | bytes 12296 | tf_op jit(solution)/shard_map/ppermute | solution.py:324
  12.1 2.3 %collective-permute-start.4 = (bf16[2,16,128,128]{3,2,1,0:T(8,128)(2,1)}, bf16[2,16,128,128]{3,2,1,0:T(8,128)(2,1)S(1)}, u32[]{:S(2)}, u32[]{:S(2)}) collective-permute-start(bf16[2,16,128,128]{3,2,1,0:T(8,128)(2,1)} %get-tuple-element.24), channel_id=1, source_target_pairs={{0,32},{32,64},{64,96},{96,128},{128,160},{160,192},{192,224},{1,3... | collective-permute-start | bytes 3145736 | tf_op jit(solution)/shard_map/ppermute | solution.py:324
  15.0 0.0 copy-done.5
  15.0 0.1 reshape.29.refs_0_
  15.1 0.0 collective-permute-done.3
  15.1 1.4 %collective-permute-done.2 = f32[8,128]{1,0:T(8,128)S(1)} collective-permute-done((f32[8,128]{1,0:T(8,128)S(1)}, f32[8,128]{1,0:T(8,128)S(1)}, u32[]{:S(2)}, u32[]{:S(2)}) %collective-permute-start.2) | collective-permute-done | bytes 4128 | tf_op jit(solution)/shard_map/ppermute | solution.py:324
  16.5 0.0 collective-permute-done.1
  16.5 3.8 %collective-permute-done.5.left_hbm = bf16[2,16,128,128]{3,2,1,0:T(8,128)(2,1)S(1)} collective-permute-done((bf16[2,16,128,128]{3,2,1,0:T(8,128)(2,1)}, bf16[2,16,128,128]{3,2,1,0:T(8,128)(2,1)S(1)}, u32[]{:S(2)}, u32[]{:S(2)}) %collective-permute-start.5) | collective-permute-done | bytes 1048608 | tf_op jit(solution)/shard_map/ppermute | solution.py:324
  20.3 0.0 copy-done.1
  20.3 0.0 copy-done.2
  20.3 0.0 copy-done.3
  20.3 12.5 %krylov.2 = (f32[1,128]{1,0:T(1,128)S(1)}, f32[2,512,128]{2,1,0:T(8,128)S(1)}, f32[2,512,128]{2,1,0:T(8,128)S(1)}, bf16[256,256]{1,0:T(8,128)(2,1)S(1)}) custom-call(s32[1,1]{1,0:T(1,128)S(6)} %copy.15.live_ref, s32[1]{0:T(128)} %bitcast.region_ref, f32[4,128]{1,0:T(4,128)S(1)} %add_select_fusion.offset_hbm, bf16[4,512,128]{2,1,0:T(8,128)(2,1)S(1)} %bitcast.17, ...), custom_call_target="tpu_custom_call" | custom-call | flops 10000000000 | bytes 4194304 | tf_op jit(solution)/shard_map/krylov/pallas_call | solution.py:357
  32.8 0.0 collective-permute-done.4.left_hbm
  32.9 0.4 krylov.3
  33.2 33.2 %all_to_all.5 = f32[32,1,128]{2,1,0:T(1,128)S(1)} all-to-all(f32[32,1,128]{2,1,0:T(1,128)S(1)} %bitcast.20), channel_id=1, replica_groups=mesh['region'=8,'sector'=32] {'sector'}, dimensions={0} | all-to-all | bytes 32768 | tf_op jit(solution)/shard_map/all_to_all | solution.py:431
  66.4 3.0 %rotate.1 = (bf16[4,512,128]{2,1,0:T(8,128)(2,1)}, f32[4,128,128]{2,1,0:T(8,128)}, f32[1,1]{1,0:T(1,128)}) custom-call(s32[1,1]{1,0:T(1,128)S(6)} %copy.15.live_ref, f32[32,128]{1,0:T(8,128)S(1)} %bitcast.21, f32[32,128]{1,0:T(8,128)S(1)} %get-tuple-element.15.own_hbm, bf16[4,512,128]{2,1,0:T(8,128)(2,1)S(1)} %bitcast.19, ...), custom_call_target="tpu_custom_call" | custom-call | tf_op jit(solution)/shard_map/rotate/pallas_call | solution.py:386
  (7 shorter events, 0.1 us)
Async XLA Ops:
  0.6 19.7 %copy-start.1 = (bf16[512,512]{1,0:T(8,128)(2,1)S(1)}, bf16[512,512]{1,0:T(8,128)(2,1)}, u32[]{:S(2)}) copy-start(bf16[512,512]{1,0:T(8,128)(2,1)} %constant.30.clone.lanes_hbm) | copy-start | bytes 1572868
  0.6 19.7 %copy-start.2 = (bf16[256,256]{1,0:T(8,128)(2,1)S(1)}, bf16[256,256]{1,0:T(8,128)(2,1)}, u32[]{:S(2)}) copy-start(bf16[256,256]{1,0:T(8,128)(2,1)} %constant.33.clone.refs_3_) | copy-start | bytes 393220
  0.7 19.7 %copy-start.3 = (bf16[256,64]{1,0:T(8,128)(2,1)S(1)}, bf16[256,64]{1,0:T(8,128)(2,1)}, u32[]{:S(2)}) copy-start(bf16[256,64]{1,0:T(8,128)(2,1)} %constant.31.clone.refs_1_) | copy-start | bytes 98308
  0.7 19.6 %copy-start.4 = (bf16[64,256]{1,0:T(8,128)(2,1)S(1)}, bf16[64,256]{1,0:T(8,128)(2,1)}, u32[]{:S(2)}) copy-start(bf16[64,256]{1,0:T(8,128)(2,1)} %constant.32.clone.refs_2_) | copy-start | bytes 98308
  0.7 5.2 %copy-start.6 = (f32[1,4,128]{2,1,0:T(4,128)S(1)}, f32[1,4,128]{2,1,0:T(4,128)}, u32[]{:S(2)}) copy-start(f32[1,4,128]{2,1,0:T(4,128)} %param.16) | copy-start | bytes 6148
  0.7 5.2 %copy-start.7 = (f32[1,4,128]{2,1,0:T(4,128)S(1)}, f32[1,4,128]{2,1,0:T(4,128)}, u32[]{:S(2)}) copy-start(f32[1,4,128]{2,1,0:T(4,128)} %param.15) | copy-start | bytes 6148
  0.7 14.3 %copy-start.5 = (bf16[16,4,4,16]{3,2,1,0:T(4,128)(2,1)S(1)}, bf16[16,4,4,16]{3,2,1,0:T(4,128)(2,1)}, u32[]{:S(2)}) copy-start(bf16[16,4,4,16]{3,2,1,0:T(4,128)(2,1)} %param.14) | copy-start | bytes 24580
  0.7 19.6 %copy-start = (bf16[1,4,128,4,128]{4,3,2,1,0:T(4,128)(2,1)S(1)}, bf16[1,4,128,4,128]{4,3,2,1,0:T(4,128)(2,1)}, u32[]{:S(2)}) copy-start(bf16[1,4,128,4,128]{4,3,2,1,0:T(4,128)(2,1)} %param.11) | copy-start | bytes 1572868
  3.9 16.4 %collective-permute-start.5 = (bf16[2,16,128,128]{3,2,1,0:T(8,128)(2,1)}, bf16[2,16,128,128]{3,2,1,0:T(8,128)(2,1)S(1)}, u32[]{:S(2)}, u32[]{:S(2)}) collective-permute-start(bf16[2,16,128,128]{3,2,1,0:T(8,128)(2,1)} %get-tuple-element.23), channel_id=1, source_target_pairs={{0,32},{32,64},{64,96},{96,128},{128,160},{160,192},{192,224},{1,3... | collective-permute-start | bytes 3145736 | tf_op jit(solution)/shard_map/ppermute | solution.py:324
  5.9 2.2 %collective-permute-start = (f32[8,128]{1,0:T(8,128)S(1)}, f32[8,128]{1,0:T(8,128)S(1)}, u32[]{:S(2)}, u32[]{:S(2)}) collective-permute-start(f32[8,128]{1,0:T(8,128)S(1)} %pad_maximum_fusion), channel_id=1, source_target_pairs={{0,32},{32,0},{64,96},{96,64},{128,160},{160,128},{192,224},{224,1... | collective-permute-start | bytes 12296 | tf_op jit(solution)/shard_map/ppermute | solution.py:330
  8.2 7.0 %collective-permute-start.3 = (f32[8,128]{1,0:T(8,128)S(1)}, f32[8,128]{1,0:T(8,128)S(1)}, u32[]{:S(2)}, u32[]{:S(2)}) collective-permute-start(f32[8,128]{1,0:T(8,128)S(1)} %pad_maximum_fusion.1), channel_id=1, source_target_pairs={{0,192},{32,224},{1,193},{33,225},{2,194},{34,226},{3,195},{35,227... | collective-permute-start | bytes 12296 | tf_op jit(solution)/shard_map/ppermute | solution.py:324
  9.5 7.0 %collective-permute-start.2 = (f32[8,128]{1,0:T(8,128)S(1)}, f32[8,128]{1,0:T(8,128)S(1)}, u32[]{:S(2)}, u32[]{:S(2)}) collective-permute-start(f32[8,128]{1,0:T(8,128)S(1)} %pad_maximum_fusion.1), channel_id=1, source_target_pairs={{0,128},{32,160},{64,192},{96,224},{1,129},{33,161},{65,193},{97,2... | collective-permute-start | bytes 12296 | tf_op jit(solution)/shard_map/ppermute | solution.py:324
  10.8 5.7 %collective-permute-start.1 = (f32[8,128]{1,0:T(8,128)S(1)}, f32[8,128]{1,0:T(8,128)S(1)}, u32[]{:S(2)}, u32[]{:S(2)}) collective-permute-start(f32[8,128]{1,0:T(8,128)S(1)} %pad_maximum_fusion.1), channel_id=1, source_target_pairs={{0,64},{32,96},{64,128},{96,160},{128,192},{160,224},{1,65},{33,97... | collective-permute-start | bytes 12296 | tf_op jit(solution)/shard_map/ppermute | solution.py:324
  12.1 20.8 %collective-permute-start.4 = (bf16[2,16,128,128]{3,2,1,0:T(8,128)(2,1)}, bf16[2,16,128,128]{3,2,1,0:T(8,128)(2,1)S(1)}, u32[]{:S(2)}, u32[]{:S(2)}) collective-permute-start(bf16[2,16,128,128]{3,2,1,0:T(8,128)(2,1)} %get-tuple-element.24), channel_id=1, source_target_pairs={{0,32},{32,64},{64,96},{96,128},{128,160},{160,192},{192,224},{1,3... | collective-permute-start | bytes 3145736 | tf_op jit(solution)/shard_map/ppermute | solution.py:324

commit v5 on v4

--- a/solution.py
+++ b/solution.py
@@ -16,7 +16,7 @@
 CHAN = 16
 ROWS = BLK * PHYS
 GROUP = 4
-VMEM_LIMIT = 50 << 20
+VMEM_LIMIT = 52 << 20
 GROUPED = 2
 STRIDE = 8
 

time: 69.9 us -> 69.9 us (level)
  blocking collectives: 33.2 us -> 21 us
  Pallas kernels: 15.9 us -> 28.1 us
    all_to_all x1, blocking collectives: 33.2 us -> 21 us  [body(): lax.all_to_all(sums.reshape(sectors, 1, BLK), 'sector', 0, 0)]
    pallas_call x2, Pallas kernels: 12.9 us -> 24.9 us  [krylov_call(): pl.pallas_call(kernel, in_specs=[SMEM, SMEM] + [HBM] * (len(operands) - 2...]
    unnamed x16 -> x18, local copies, waits for them, and re-layouts: 0.04 us -> 1.63 us
    squeeze x1, local copies, waits for them, and re-layouts: 3.22 us -> 1.89 us  [body(): left_env[0, at:at + GROUPED]]
where the time goes in v5:
time: 69.9 us; the launch traced here: 69.8 us
  Pallas kernels  28.1 us (40%)
  blocking collectives  21 us (30%)
  starting transfers between devices  8.18 us (12%)
  waiting for transfers between devices  7.18 us (10%)
  local copies, waits for them, and re-layouts  3.62 us (5%)
  between operations  1.66 us (2%)
    pallas_call x2, Pallas kernels, krylov_call(): pl.pallas_call(kernel, in_specs=[SMEM, SMEM] + [HBM] * (len(operands) - 2...  24.9 us
    all_to_all x1, blocking collectives, body(): lax.all_to_all(sums.reshape(sectors, 1, BLK), 'sector', 0, 0)  21 us
    ppermute x5, starting transfers between devices, from_behind(): return lax.ppermute(shard, axis, [(i, i + by) for i in range(length - by)])  8.09 us
    ppermute x5, waiting for transfers between devices, from_behind(): return lax.ppermute(shard, axis, [(i, i + by) for i in range(length - by)])  5.06 us
    pallas_call x1, Pallas kernels, rotate_call(): pl.pallas_call(functools.partial(rotate_kernel, math.sqrt(slots * sectors...  3.25 us
    ppermute x1, waiting for transfers between devices, entering(): lax.ppermute(own, axis, [(i, i ^ 1) for i in range(lax.axis_size(axis))])  2.12 us
    squeeze x1, local copies, waits for them, and re-layouts, body(): left_env[0, at:at + GROUPED]  1.89 us
    unnamed x18, local copies, waits for them, and re-layouts  1.63 us
  transfers between devices with their start and end apart: 6, of which 3 were waited for; matrix products, arithmetic and copies ran while one was open for 0% of the time, Pallas kernels for 18%

profile of v5, /device:TPU:6, one launch (start us, length us, event | category | flops | bytes accessed | tf_op | source)
XLA Modules:
  0.0 69.8 jit_solution(767295295696500835)
XLA Ops:
  0.6 0.0 copy-start.3
  0.6 0.0 copy-start.4
  0.7 0.0 copy-start.5
  0.7 0.0 copy-start.7
  0.7 0.0 copy-start.8
  0.7 0.0 copy-start.6
  0.7 0.0 copy-start
  0.7 1.9 %slice_bitcast_fusion = (bf16[2,16,128,128]{3,2,1,0:T(8,128)(2,1)S(1)}, bf16[2,16,128,128]{3,2,1,0:T(8,128)(2,1)S(1)}) fusion(bf16[1,4,16,128,128]{4,3,2,1,0:T(8,128)(2,1)} %param.12), kind=kLoop, calls=%fused_computation | loop fusion | bytes 4194304 | tf_op jit(solution)/shard_map/squeeze | solution.py:414
  2.6 1.9 %collective-permute-start.5 = (bf16[2,16,128,128]{3,2,1,0:T(8,128)(2,1)S(1)}, bf16[2,16,128,128]{3,2,1,0:T(8,128)(2,1)}, u32[]{:S(2)}, u32[]{:S(2)}) collective-permute-start(bf16[2,16,128,128]{3,2,1,0:T(8,128)(2,1)S(1)} %get-tuple-element.23), channel_id=1, source_target_pairs={{0,32},{32,64},{64,96},{96,128},{128,160},{160,192},{192,224},{1,3... | collective-permute-start | bytes 3145736 | tf_op jit(solution)/shard_map/ppermute | solution.py:324
  4.5 0.0 copy-done.7
  4.5 0.0 copy-done.8
  4.6 0.1 collective-permute-start
  4.7 2.1 %collective-permute-done = f32[8,128]{1,0:T(8,128)S(1)} collective-permute-done((f32[8,128]{1,0:T(8,128)S(1)}, f32[8,128]{1,0:T(8,128)S(1)}, u32[]{:S(2)}, u32[]{:S(2)}) %collective-permute-start) | collective-permute-done | bytes 4128 | tf_op jit(solution)/shard_map/ppermute | solution.py:330
  6.8 1.3 %collective-permute-start.3 = (f32[8,128]{1,0:T(8,128)S(1)}, f32[8,128]{1,0:T(8,128)S(1)}, u32[]{:S(2)}, u32[]{:S(2)}) collective-permute-start(f32[8,128]{1,0:T(8,128)S(1)} %pad_maximum_fusion.1), channel_id=1, source_target_pairs={{0,192},{32,224},{1,193},{33,225},{2,194},{34,226},{3,195},{35,227... | collective-permute-start | bytes 12296 | tf_op jit(solution)/shard_map/ppermute | solution.py:324
  8.1 1.3 %collective-permute-start.2 = (f32[8,128]{1,0:T(8,128)S(1)}, f32[8,128]{1,0:T(8,128)S(1)}, u32[]{:S(2)}, u32[]{:S(2)}) collective-permute-start(f32[8,128]{1,0:T(8,128)S(1)} %pad_maximum_fusion.1), channel_id=1, source_target_pairs={{0,128},{32,160},{64,192},{96,224},{1,129},{33,161},{65,193},{97,2... | collective-permute-start | bytes 12296 | tf_op jit(solution)/shard_map/ppermute | solution.py:324
  9.4 1.3 %collective-permute-start.1 = (f32[8,128]{1,0:T(8,128)S(1)}, f32[8,128]{1,0:T(8,128)S(1)}, u32[]{:S(2)}, u32[]{:S(2)}) collective-permute-start(f32[8,128]{1,0:T(8,128)S(1)} %pad_maximum_fusion.1), channel_id=1, source_target_pairs={{0,64},{32,96},{64,128},{96,160},{128,192},{160,224},{1,65},{33,97... | collective-permute-start | bytes 12296 | tf_op jit(solution)/shard_map/ppermute | solution.py:324
  10.7 2.3 %collective-permute-start.4 = (bf16[2,16,128,128]{3,2,1,0:T(8,128)(2,1)S(1)}, bf16[2,16,128,128]{3,2,1,0:T(8,128)(2,1)}, u32[]{:S(2)}, u32[]{:S(2)}) collective-permute-start(bf16[2,16,128,128]{3,2,1,0:T(8,128)(2,1)S(1)} %get-tuple-element.24), channel_id=1, source_target_pairs={{0,32},{32,64},{64,96},{96,128},{128,160},{160,192},{192,224},{1,3... | collective-permute-start | bytes 3145736 | tf_op jit(solution)/shard_map/ppermute | solution.py:324
  13.7 0.0 copy-done.6
  13.7 0.1 reshape.29.refs_0_
  13.8 0.0 collective-permute-done.3
  13.8 1.4 %collective-permute-done.2 = f32[8,128]{1,0:T(8,128)S(1)} collective-permute-done((f32[8,128]{1,0:T(8,128)S(1)}, f32[8,128]{1,0:T(8,128)S(1)}, u32[]{:S(2)}, u32[]{:S(2)}) %collective-permute-start.2) | collective-permute-done | bytes 4128 | tf_op jit(solution)/shard_map/ppermute | solution.py:324
  15.2 0.0 collective-permute-done.1
  15.2 3.7 %collective-permute-done.5.left_hbm = bf16[2,16,128,128]{3,2,1,0:T(8,128)(2,1)} collective-permute-done((bf16[2,16,128,128]{3,2,1,0:T(8,128)(2,1)S(1)}, bf16[2,16,128,128]{3,2,1,0:T(8,128)(2,1)}, u32[]{:S(2)}, u32[]{:S(2)}) %collective-permute-start.5) | collective-permute-done | bytes 1048608 | tf_op jit(solution)/shard_map/ppermute | solution.py:324
  18.9 0.0 copy-done.3
  18.9 0.0 copy-done.4
  18.9 12.5 %krylov.2 = (f32[1,128]{1,0:T(1,128)S(1)}, f32[2,512,128]{2,1,0:T(8,128)S(1)}, f32[2,512,128]{2,1,0:T(8,128)S(1)}, bf16[256,256]{1,0:T(8,128)(2,1)S(1)}) custom-call(s32[1,1]{1,0:T(1,128)S(6)} %copy.15.live_ref, s32[1]{0:T(128)} %bitcast.region_ref, f32[4,128]{1,0:T(4,128)S(1)} %add_select_fusion.offset_hbm, bf16[4,512,128]{2,1,0:T(8,128)(2,1)S(1)} %bitcast.17, ...), custom_call_target="tpu_custom_call" | custom-call | flops 10000000000 | bytes 4194304 | tf_op jit(solution)/shard_map/krylov/pallas_call | solution.py:357
  31.4 0.8 %copy-done.1 = f32[2,512,128]{2,1,0:T(8,128)} copy-done((f32[2,512,128]{2,1,0:T(8,128)}, f32[2,512,128]{2,1,0:T(8,128)S(1)}, u32[]{:S(2)}) %copy-start.1) | copy-done | bytes 524312
  32.2 0.0 collective-permute-done.4.left_hbm
  32.2 12.3 %krylov.3 = (f32[32,128]{1,0:T(8,128)S(1)}, f32[2,512,128]{2,1,0:T(8,128)S(1)}, f32[2,512,128]{2,1,0:T(8,128)S(1)}) custom-call(s32[1,1]{1,0:T(1,128)S(6)} %copy.15.live_ref, s32[1]{0:T(128)} %bitcast.region_ref, f32[4,128]{1,0:T(4,128)S(1)} %add_select_fusion.offset_hbm, bf16[4,512,128]{2,1,0:T(8,128)(2,1)S(1)} %bitcast.18, ...), custom_call_target="tpu_custom_call" | custom-call | flops 10000000000 | bytes 4194304 | tf_op jit(solution)/shard_map/krylov/pallas_call | solution.py:357
  44.6 0.8 %copy-done.2 = f32[2,512,128]{2,1,0:T(8,128)} copy-done((f32[2,512,128]{2,1,0:T(8,128)}, f32[2,512,128]{2,1,0:T(8,128)S(1)}, u32[]{:S(2)}) %copy-start.2) | copy-done | bytes 524312
  45.4 21.0 %all_to_all.5 = f32[32,1,128]{2,1,0:T(1,128)S(1)} all-to-all(f32[32,1,128]{2,1,0:T(1,128)S(1)} %bitcast.20), channel_id=1, replica_groups=mesh['region'=8,'sector'=32] {'sector'}, dimensions={0} | all-to-all | bytes 32768 | tf_op jit(solution)/shard_map/all_to_all | solution.py:431
  66.4 3.2 %rotate.1 = (bf16[4,512,128]{2,1,0:T(8,128)(2,1)}, f32[4,128,128]{2,1,0:T(8,128)}, f32[1,1]{1,0:T(1,128)}) custom-call(s32[1,1]{1,0:T(1,128)S(6)} %copy.15.live_ref, f32[32,128]{1,0:T(8,128)S(1)} %bitcast.21, f32[32,128]{1,0:T(8,128)S(1)} %get-tuple-element.15.own_hbm, bf16[4,512,128]{2,1,0:T(8,128)(2,1)S(1)} %bitcast.19, ...), custom_call_target="tpu_custom_call" | custom-call | tf_op jit(solution)/shard_map/rotate/pallas_call | solution.py:386
  (9 shorter events, 0.1 us)
Async XLA Ops:
  0.6 18.2 %copy-start.3 = (bf16[256,256]{1,0:T(8,128)(2,1)S(1)}, bf16[256,256]{1,0:T(8,128)(2,1)}, u32[]{:S(2)}) copy-start(bf16[256,256]{1,0:T(8,128)(2,1)} %constant.33.clone.refs_3_) | copy-start | bytes 393220
  0.6 18.2 %copy-start.4 = (bf16[256,64]{1,0:T(8,128)(2,1)S(1)}, bf16[256,64]{1,0:T(8,128)(2,1)}, u32[]{:S(2)}) copy-start(bf16[256,64]{1,0:T(8,128)(2,1)} %constant.31.clone.refs_1_) | copy-start | bytes 98308
  0.7 18.2 %copy-start.5 = (bf16[64,256]{1,0:T(8,128)(2,1)S(1)}, bf16[64,256]{1,0:T(8,128)(2,1)}, u32[]{:S(2)}) copy-start(bf16[64,256]{1,0:T(8,128)(2,1)} %constant.32.clone.refs_2_) | copy-start | bytes 98308
  0.7 3.9 %copy-start.7 = (f32[1,4,128]{2,1,0:T(4,128)S(1)}, f32[1,4,128]{2,1,0:T(4,128)}, u32[]{:S(2)}) copy-start(f32[1,4,128]{2,1,0:T(4,128)} %param.16) | copy-start | bytes 6148
  0.7 3.9 %copy-start.8 = (f32[1,4,128]{2,1,0:T(4,128)S(1)}, f32[1,4,128]{2,1,0:T(4,128)}, u32[]{:S(2)}) copy-start(f32[1,4,128]{2,1,0:T(4,128)} %param.15) | copy-start | bytes 6148
  0.7 13.0 %copy-start.6 = (bf16[16,4,4,16]{3,2,1,0:T(4,128)(2,1)S(1)}, bf16[16,4,4,16]{3,2,1,0:T(4,128)(2,1)}, u32[]{:S(2)}) copy-start(bf16[16,4,4,16]{3,2,1,0:T(4,128)(2,1)} %param.14) | copy-start | bytes 24580
  0.7 18.2 %copy-start = (bf16[1,4,128,4,128]{4,3,2,1,0:T(4,128)(2,1)S(1)}, bf16[1,4,128,4,128]{4,3,2,1,0:T(4,128)(2,1)}, u32[]{:S(2)}) copy-start(bf16[1,4,128,4,128]{4,3,2,1,0:T(4,128)(2,1)} %param.11) | copy-start | bytes 1572868
  2.6 16.3 %collective-permute-start.5 = (bf16[2,16,128,128]{3,2,1,0:T(8,128)(2,1)S(1)}, bf16[2,16,128,128]{3,2,1,0:T(8,128)(2,1)}, u32[]{:S(2)}, u32[]{:S(2)}) collective-permute-start(bf16[2,16,128,128]{3,2,1,0:T(8,128)(2,1)S(1)} %get-tuple-element.23), channel_id=1, source_target_pairs={{0,32},{32,64},{64,96},{96,128},{128,160},{160,192},{192,224},{1,3... | collective-permute-start | bytes 3145736 | tf_op jit(solution)/shard_map/ppermute | solution.py:324
  4.6 2.2 %collective-permute-start = (f32[8,128]{1,0:T(8,128)S(1)}, f32[8,128]{1,0:T(8,128)S(1)}, u32[]{:S(2)}, u32[]{:S(2)}) collective-permute-start(f32[8,128]{1,0:T(8,128)S(1)} %pad_maximum_fusion), channel_id=1, source_target_pairs={{0,32},{32,0},{64,96},{96,64},{128,160},{160,128},{192,224},{224,1... | collective-permute-start | bytes 12296 | tf_op jit(solution)/shard_map/ppermute | solution.py:330
  6.8 7.0 %collective-permute-start.3 = (f32[8,128]{1,0:T(8,128)S(1)}, f32[8,128]{1,0:T(8,128)S(1)}, u32[]{:S(2)}, u32[]{:S(2)}) collective-permute-start(f32[8,128]{1,0:T(8,128)S(1)} %pad_maximum_fusion.1), channel_id=1, source_target_pairs={{0,192},{32,224},{1,193},{33,225},{2,194},{34,226},{3,195},{35,227... | collective-permute-start | bytes 12296 | tf_op jit(solution)/shard_map/ppermute | solution.py:324
  8.1 7.0 %collective-permute-start.2 = (f32[8,128]{1,0:T(8,128)S(1)}, f32[8,128]{1,0:T(8,128)S(1)}, u32[]{:S(2)}, u32[]{:S(2)}) collective-permute-start(f32[8,128]{1,0:T(8,128)S(1)} %pad_maximum_fusion.1), channel_id=1, source_target_pairs={{0,128},{32,160},{64,192},{96,224},{1,129},{33,161},{65,193},{97,2... | collective-permute-start | bytes 12296 | tf_op jit(solution)/shard_map/ppermute | solution.py:324
  9.4 5.7 %collective-permute-start.1 = (f32[8,128]{1,0:T(8,128)S(1)}, f32[8,128]{1,0:T(8,128)S(1)}, u32[]{:S(2)}, u32[]{:S(2)}) collective-permute-start(f32[8,128]{1,0:T(8,128)S(1)} %pad_maximum_fusion.1), channel_id=1, source_target_pairs={{0,64},{32,96},{64,128},{96,160},{128,192},{160,224},{1,65},{33,97... | collective-permute-start | bytes 12296 | tf_op jit(solution)/shard_map/ppermute | solution.py:324
  10.7 21.5 %collective-permute-start.4 = (bf16[2,16,128,128]{3,2,1,0:T(8,128)(2,1)S(1)}, bf16[2,16,128,128]{3,2,1,0:T(8,128)(2,1)}, u32[]{:S(2)}, u32[]{:S(2)}) collective-permute-start(bf16[2,16,128,128]{3,2,1,0:T(8,128)(2,1)S(1)} %get-tuple-element.24), channel_id=1, source_target_pairs={{0,32},{32,64},{64,96},{96,128},{128,160},{160,192},{192,224},{1,3... | collective-permute-start | bytes 3145736 | tf_op jit(solution)/shard_map/ppermute | solution.py:324
  31.4 0.8 %copy-start.1 = (f32[2,512,128]{2,1,0:T(8,128)}, f32[2,512,128]{2,1,0:T(8,128)S(1)}, u32[]{:S(2)}) copy-start(f32[2,512,128]{2,1,0:T(8,128)S(1)} %get-tuple-element.18.refs_2_) | copy-start | bytes 1572868
  44.6 0.8 %copy-start.2 = (f32[2,512,128]{2,1,0:T(8,128)}, f32[2,512,128]{2,1,0:T(8,128)S(1)}, u32[]{:S(2)}) copy-start(f32[2,512,128]{2,1,0:T(8,128)S(1)} %get-tuple-element.19.refs_3_) | copy-start | bytes 1572868
